TPU v7x, 256 devices: a whole 4x4x8 slice. The times are simulated.
256 devices in a mesh: lat: 4 (over x), lon: 64 (over z, y, core).
Axes of the slice: x: 4, y: 4, z: 8, core: 2. Of those that a mesh axis runs over, the one named last changes fastest.
Arguments:
- field: float32 [1024, 8640], P('lat', 'lon'), may hold values from -6 to 6
- quad_weight: float32 [1024], P('lat'), may hold values from 0.2 to 1
- legendre: bfloat16 [512, 1025, 1024], P('lon', None, 'lat'), may hold values from -0.75 to 0.75
- love_factor: float32 [1024], replicated, may hold values from 0.1 to 1
- pair_table: int32 [512], P('lon'), may hold values from 0 to 511, each once
Outputs:
- sal_field: float32 [1024, 8640], P('lat', 'lon')
Inputs may be any that keep to these rules, and one draw needn't show every extreme that they name: `pair_table`: each pair number stands once; pair p holds the orders p and 1023 - p.
All inputs are finite; a program needn't handle non-finite values.
Results may differ from a plain program's by a relative error of at most 0.0047.
Values may be sent and summed in bfloat16 or wider, within the bound.
A program may use at most 64 MiB of HBM per device.

v0:
```python
import jax
import jax.numpy as jnp
from jax import lax
from jax.sharding import PartitionSpec as P

full_turn = 6.283185307179586


def angle_tables(orders, cell_ids, length):
    turn_count = orders[..., None] * cell_ids % length
    phase_angle = turn_count.astype(jnp.float32) * (full_turn / length)
    return (jnp.cos(phase_angle), jnp.sin(phase_angle))


def per_device(field, quad_weight, legendre, love_factor, pair_table):
    lat_rows, lon_cols = field.shape
    pair_slots, packed, _ = legendre.shape
    degrees = love_factor.shape[0]
    groups = lax.axis_size("lon")
    total_lon = lon_cols * groups
    lon_index = lax.axis_index("lon")
    columns = lon_index * lon_cols + jnp.arange(lon_cols, dtype=jnp.int32)
    all_pairs = lax.all_gather(pair_table, "lon", axis=0, tiled=True)
    all_orders = jnp.stack([all_pairs, degrees - 1 - all_pairs], axis=1)
    orders = all_orders
    cos_table, sin_table = angle_tables(orders, columns, total_lon)
    real_part = jnp.einsum("spb,lb->spl", cos_table, field, precision=lax.Precision.HIGHEST)
    imag_part = -jnp.einsum("spb,lb->spl", sin_table, field, precision=lax.Precision.HIGHEST)
    stacked = jnp.stack(
        [real_part[:, 0], imag_part[:, 0], real_part[:, 1], imag_part[:, 1]], axis=1
    )
    summed = lax.psum_scatter(stacked / total_lon, "lon", scatter_dimension=0, tiled=True)
    fourier = (summed * quad_weight).astype(jnp.bfloat16)
    position = jnp.arange(packed, dtype=jnp.int32)
    low_mask = position[None, :] < (degrees - pair_table)[:, None]
    both_parts = jnp.einsum("sjl,scl->sjc", fourier, legendre, preferred_element_type=jnp.float32)
    coefficient = jnp.where(low_mask[:, None, :], both_parts[:, 0:2], both_parts[:, 2:4])
    coefficient = lax.psum(coefficient, "lat")
    padded = jnp.concatenate(
        [jnp.zeros((1,), jnp.float32), love_factor, jnp.zeros((packed + 1,), jnp.float32)]
    )
    low_love = jax.vmap(
        lambda pair_index: lax.dynamic_slice_in_dim(padded, pair_index + 1, packed)
    )(pair_table)
    factor = jnp.where(low_mask, low_love, padded[:packed][None, :])
    spectral = (coefficient * factor[:, None, :]).astype(jnp.bfloat16)
    blank_part = jnp.zeros_like(spectral)
    split_parts = jnp.concatenate(
        [
            jnp.where(low_mask[:, None, :], spectral, blank_part),
            jnp.where(low_mask[:, None, :], blank_part, spectral),
        ],
        axis=1,
    )
    order_fields = jnp.einsum(
        "sjc,scl->sjl", split_parts, legendre, preferred_element_type=jnp.float32
    ).astype(jnp.bfloat16)
    shard_piece = lax.all_gather(order_fields, "lon", axis=0, tiled=True)
    piece_rows = shard_piece.shape[0]
    orders = all_orders
    cos_table, sin_table = angle_tables(orders, columns, total_lon)
    order_scale = jnp.where(orders == 0, 1.0, 2.0).astype(jnp.float32)
    values = shard_piece.astype(jnp.float32).reshape(piece_rows, 2, 2, lat_rows)
    real_part = values[:, :, 0] * order_scale[..., None]
    imag_part = values[:, :, 1] * order_scale[..., None]
    added = jnp.einsum("spl,spb->lb", real_part, cos_table, precision=lax.Precision.HIGHEST)
    taken = jnp.einsum("spl,spb->lb", imag_part, sin_table, precision=lax.Precision.HIGHEST)
    return added - taken


def solution(mesh):
    placed = (P("lat", "lon"), P("lat"), P("lon", None, "lat"), P(), P("lon"))
    return jax.shard_map(
        per_device, mesh=mesh, in_specs=placed, out_specs=P("lat", "lon"), check_vma=False
    )
```

profile of v0, /device:TPU:1, one launch (start us, length us, event | category | flops | bytes accessed | tf_op | source)
XLA Modules:
  0.0 327.7 jit_solution(15728099518413216490)
XLA Ops:
  6.5 1.3 dynamic-slice.3
  8.5 0.9 dynamic-update-slice.2
  9.4 20.7 %all-reduce = s32[512]{0:T(512)S(1)} all-reduce(s32[512]{0:T(512)S(1)} %dynamic-update-slice.2), channel_id=1, replica_groups=mesh['lat'=4,'lon'=64] {'lon'}, use_global_device_ids=true, to_apply=%add | all-reduce | flops 512 | bytes 4096
  30.1 3.8 %convolution_negate_fusion = f32[512,2,256]{2,0,1:T(8,128)S(1)} fusion(s32[135]{0:T(256)S(1)} %iota_add_fusion, s32[512,2]{0,1:T(2,128)S(1)} %pad_add_fusion, f32[256,135]{0,1:T(8,128)S(1)} %copy-done), kind=kOutput, calls=%fused_computation.6 | convolution fusion | flops 426179584 | bytes 1191452 | tf_op jit(solution)/shard_map/spb,lb->spl/dot_general | solution.py:28
  34.0 3.8 %fusion.19 = f32[512,2,256]{2,0,1:T(8,128)S(1)} fusion(s32[135]{0:T(256)S(1)} %iota_add_fusion, s32[512,2]{0,1:T(2,128)S(1)} %pad_add_fusion, f32[256,135]{0,1:T(8,128)S(1)} %copy-done), kind=kOutput, calls=%fused_computation.23 | convolution fusion | flops 425917440 | bytes 1191452 | tf_op jit(solution)/shard_map/spb,lb->spl/dot_general | solution.py:27
  37.8 0.1 fusion.67
  37.9 1.5 maximum_multiply_fusion
  39.5 0.6 copy-done.1
  40.1 0.1 concatenate.13
  40.2 12.2 %while.1 = (s32[]{:T(128)}, f32[2051]{0:T(1024)S(1)}, s32[8,1]{0,1:T(1,128)S(1)}, f32[8,1025]{1,0:T(8,128)S(1)}, s32[]{:T(128)}, /*index=5*/s32[]{:T(128)}) while((s32[]{:T(128)}, f32[2051]{0:T(1024)S(1)}, s32[8,1]{0,1:T(1,128)S(1)}, f32[8,1025]{1,0:T(8,128)S(1)}, s32[]{:T(128)}, /*index=5*/s32[]{:T(128)}) %tuple.23), condition=%wide.while_cond, body=%wide.while_body.sunk | while | flops 2 | bytes 24689 | solution.py:43
  40.2 0.7 constant_dynamic-slice_fusion.2
  40.9 0.8 dynamic-slice.8
  41.6 0.1 dynamic-update-slice.4
  41.7 0.7 constant_dynamic-slice_fusion.2
  42.4 0.8 dynamic-slice.8
  43.2 0.1 dynamic-update-slice.4
  43.3 0.7 constant_dynamic-slice_fusion.2
  43.9 0.8 dynamic-slice.8
  44.7 0.1 dynamic-update-slice.4
  44.8 0.7 constant_dynamic-slice_fusion.2
  45.5 0.8 dynamic-slice.8
  46.2 0.1 dynamic-update-slice.4
  46.3 0.7 constant_dynamic-slice_fusion.2
  47.0 0.8 dynamic-slice.8
  47.7 0.1 dynamic-update-slice.4
  47.9 0.7 constant_dynamic-slice_fusion.2
  48.5 0.8 dynamic-slice.8
  49.3 0.1 dynamic-update-slice.4
  49.4 0.7 constant_dynamic-slice_fusion.2
  50.0 0.8 dynamic-slice.8
  50.8 0.1 dynamic-update-slice.4
  50.9 0.7 constant_dynamic-slice_fusion.2
  51.6 0.8 dynamic-slice.8
  52.3 0.1 dynamic-update-slice.4
  52.5 0.1 iota_compare_fusion
  52.6 121.5 %reduce-scatter.2.cloned.1.call-done = f32[8,4,256]{2,0,1:T(8,128)} async-done(((f32[512,4,256]{2,0,1:T(8,128)}), f32[8,4,256]{2,0,1:T(8,128)}) %reduce-scatter.2.cloned.1.call-update) | async-done | bytes 32784 | tf_op jit(solution)/shard_map/reduce_scatter | solution.py:32
  174.1 0.8 multiply_convert_fusion.1
  174.8 3.4 %fusion.2 = f32[8,4,1025]{2,1,0:T(4,128)S(1)} fusion(bf16[8,1025,256]{2,0,1:T(8,128)(2,1)} %param.7, bf16[8,4,256]{2,0,1:T(8,128)(2,1)S(1)} %multiply_convert_fusion.1), kind=kOutput, calls=%fused_computation.3 | convolution fusion | flops 16793600 | bytes 4345984 | tf_op jit(solution)/shard_map/sjl,scl->sjc/dot_general | solution.py:36
  178.3 0.7 slice_select_fusion
  179.0 0.2 all-gather.2.cloned.1.call-start
  179.3 46.7 %all-reduce.3.cloned.1.call-done = f32[8,2,1025]{2,1,0:T(2,128)} async-done(((f32[8,2,1025]{2,1,0:T(2,128)}), f32[8,2,1025]{2,1,0:T(2,128)}) %all-reduce.3.cloned.1.call-update) | async-done | bytes 65616 | tf_op jit(solution)/shard_map/psum | solution.py:38
  226.0 1.0 broadcast_select_fusion.1
  227.0 3.6 %fusion.5 = bf16[8,4,256]{2,1,0:T(4,128)(2,1)} fusion(bf16[8,1025,256]{2,0,1:T(8,128)(2,1)} %param.7, bf16[8,2,1025]{2,1,0:T(2,128)(2,1)S(1)} %get-tuple-element.28, bf16[8,2,1025]{2,1,0:T(2,128)(2,1)S(1)} %get-tuple-element.27), kind=kOutput, calls=%fused_computation.10 | convolution fusion | flops 16932992 | bytes 4280384 | tf_op jit(solution)/shard_map/sjc,scl->sjl/dot_general | solution.py:55
  230.6 79.8 %all-gather.2.cloned.1.call-done = bf16[512,4,256]{2,1,0:T(4,128)(2,1)} async-done(((bf16[8,4,256]{2,1,0:T(4,128)(2,1)}), bf16[512,4,256]{2,1,0:T(4,128)(2,1)}) %all-gather.2.cloned.1.call-update) | async-done | bytes 1048592 | tf_op jit(solution)/shard_map/all_gather | solution.py:58
  310.3 2.5 reshape.91
  312.9 1.6 fusion.66
  314.5 3.0 convolution_bitcast_fusion
  317.5 3.6 %fusion.4 = f32[256,135]{0,1:T(8,128)} fusion(f32[256,135]{0,1:T(8,128)S(1)} %convolution_bitcast_fusion, f32[512,2,1,256]{3,2,1,0:T(1,128)S(1)} %get-tuple-element.21, f32[512,2]{0,1:T(2,128)S(1)} %compare_select_fusion, s32[135]{0:T(256)S(1)} %iota_add_fusion, s32[512,2]{0,1:T(2,128)S(1)} %pad_add_fusion), kind=kOutput, calls=%fused_computation.9 | convolution fusion | flops 426214144 | bytes 1333788 | tf_op jit(solution)/shard_map/spl,spb->lb/dot_general | solution.py:66
  (30 shorter events, 0.3 us)
Async XLA Ops:
  6.5 23.6 %copy-start = (f32[256,135]{0,1:T(8,128)S(1)}, f32[256,135]{0,1:T(8,128)}, u32[]{:S(2)}) copy-start(f32[256,135]{0,1:T(8,128)} %param.5) | copy-start | bytes 414724
  6.5 167.5 %reduce-scatter.2.cloned.1.call-start = ((), (), s32[]{:S(2)}) async-start(), calls=%async_computation.1 | async-start | bytes 2129920 | tf_op jit(solution)/shard_map/reduce_scatter | solution.py:32
  39.4 0.7 copy-start.1
  39.4 0.8 copy-start.3
  39.4 134.6 %copy-start.2 = (f32[256]{0:T(256)S(1)}, f32[256]{0:T(256)}, u32[]{:S(2)}) copy-start(f32[256]{0:T(256)} %param.6) | copy-start | bytes 3076
  39.5 186.5 %all-reduce.3.cloned.1.call-start = ((), (), s32[]{:S(2)}) async-start(), calls=%async_computation.2 | async-start | bytes 147456 | tf_op jit(solution)/shard_map/psum | solution.py:38
  179.0 131.4 %all-gather.2.cloned.1.call-start = ((), (), s32[]{:S(2)}) async-start(), calls=%async_computation.3 | async-start | bytes 1064960 | tf_op jit(solution)/shard_map/all_gather | solution.py:58
Sparse Core Ops, SparseCore 0:
  39.6 134.4 reduce-scatter.1
  179.1 46.8 all-reduce.2
  230.7 79.6 all-gather.1
where the time goes:
time: 328 us
  waiting for transfers between devices  248 us (76%)
  matrix products  21.2 us (6%)
  blocking collectives  20.7 us (6%)
  local copies, waits for them, and re-layouts  19.2 us (6%)
  between operations  13.9 us (4%)
  other arithmetic  4.23 us (1%)
    reduce_scatter x1, waiting for transfers between devices, per_device(): lax.psum_scatter(stacked / total_lon, 'lon', scatter_dimension=0, tiled=T...  121 us
    all_gather x1, waiting for transfers between devices, per_device(): shard_piece = lax.all_gather(order_fields, 'lon', axis=0, tiled=True)  79.8 us
    psum x1, waiting for transfers between devices, per_device(): coefficient = lax.psum(coefficient, 'lat')  46.7 us
    unnamed x1, blocking collectives  20.7 us
    gather x32, local copies, waits for them, and re-layouts  12 us
  transfers between devices with their start and end apart: 3, of which 3 were waited for; matrix products, arithmetic and copies ran while one was open for 4% of the time, Pallas kernels for 0%

commit v1 on v0

v1 whole, which is shorter than its diff:
```python
import math

import jax
import jax.numpy as jnp
import ml_dtypes
import numpy as np
from jax import lax
from jax.experimental import pallas as pl
from jax.experimental.pallas import tpu as pltpu
from jax.sharding import PartitionSpec as P

F32 = jnp.float32
BF16 = jnp.bfloat16
TOTAL_LON = 8640
LON_COLS = 135
DEGREES = 1024
GROUPS = ((0, 4), (1, 7), (2, 6), (3, 5))
FAR_FIRST = (4, 3, 5, 2, 6, 1, 7)


def pair_orders():
    steps = 8 * np.arange(64)
    low = np.concatenate([steps + r for group in GROUPS for r in group])
    high = np.concatenate([steps + 7 - r for group in GROUPS for r in group])
    return low, high


def angle_constants():
    low, high = pair_orders()
    columns = np.arange(LON_COLS)
    made = np.zeros((8, 4, 2, 512, 256), ml_dtypes.bfloat16)
    for group in range(4):
        span = slice(128 * group, 128 * group + 128)
        orders = np.concatenate([low[span], DEGREES - 1 - high[span]])
        sign = np.ones((256, 1))
        if group:
            sign[64:128] = -1.0
            sign[192:256] = -1.0
        for q in range(8):
            turns = orders[:, None] * (LON_COLS * q + columns) % TOTAL_LON
            angle = turns * (2.0 * np.pi / TOTAL_LON)
            both = np.concatenate([np.cos(angle), np.sin(angle) * sign])
            head = both.astype(ml_dtypes.bfloat16)
            made[q, group, 0, :, :LON_COLS] = head
            made[q, group, 1, :, :LON_COLS] = (both - head.astype(np.float64)).astype(ml_dtypes.bfloat16)
    return made


def kernel(
    field, quad, love, pairs, perm, legendre, angles, out,
    leg, table, tail, last_rows, s1, r1, rp1, rp2, onehot, rhs, orders_all, s2, r2, s3, r3, four, s4, r4, r5,
    factor, love_rows, blocks, s6, r6, r7, s8, r8,
    local_sem, sem_pz, sem_pq, sem1, sem2, sem3, sem4, sem5, sem6, sem7, sem8,
):
    lon = lax.axis_index("lon")
    x = lax.axis_index("lat")
    z = lon // 8
    q = lon % 8

    def z_device(i):
        return {"lon": i * 8 + q}

    def q_device(i):
        return {"lon": z * 8 + i}

    def x_device(i):
        return {"lat": i}

    barrier = pltpu.get_barrier_semaphore()
    for d in range(1, 8):
        pl.semaphore_signal(barrier, inc=1, device_id=z_device((z + d) % 8))
        pl.semaphore_signal(barrier, inc=1, device_id=q_device((q + d) % 8))
    for d in range(1, 4):
        pl.semaphore_signal(barrier, inc=1, device_id=x_device((x + d) % 4))

    leg_copy = pltpu.make_async_copy(legendre, leg, local_sem.at[0])
    table_copy = pltpu.make_async_copy(angles.at[q], table, local_sem.at[1])
    leg_copy.start()
    table_copy.start()

    started = []

    def send(distances, me, size, device, source, target, sems):
        copies = []
        for d in distances:
            to = (me + d) % size
            copy = pltpu.make_async_remote_copy(
                src_ref=source(to), dst_ref=target(d),
                send_sem=sems.at[0, d], recv_sem=sems.at[1, d],
                device_id=device(to),
            )
            copy.start()
            copies.append(copy)
        started.extend(copies)
        return copies

    def arrive(copies):
        for copy in copies:
            copy.wait_recv()

    lane = lax.broadcasted_iota(jnp.int32, (1, 128), 1)
    quarter = lane // 32
    step_in_tile = lane // 8

    last_rows[...] = jnp.zeros_like(last_rows)
    last_rows[0:15, :] = field[120:135, :]
    for h in range(2):
        cols = slice(128 * h, 128 * h + 128)
        runs = [field[40 * c:40 * c + 40, cols] for c in range(3)] + [last_rows[:, cols]]
        for g in range(4):
            packed = pltpu.roll(runs[0], (32 * (0 - g)) % 128, 1) if g else runs[0]
            for c in range(1, 4):
                moved = pltpu.roll(runs[c], (32 * (c - g)) % 128, 1) if c != g else runs[c]
                packed = jnp.where(quarter == c, moved, packed)
            s1[4 * h + g] = packed

    pl.semaphore_wait(barrier, 17)
    copies_pz = send(FAR_FIRST, z, 8, z_device, lambda to: pairs, lambda d: rp1.at[z], sem_pz)
    copies1 = send(FAR_FIRST, z, 8, z_device, lambda to: s1.at[to], lambda d: r1.at[z], sem1)
    r1[z] = s1[z]
    rp1[z] = pairs[...]

    pair_lane = pairs[0:1, :]
    rhs[...] = jnp.zeros_like(rhs)
    s4[...] = jnp.zeros_like(s4)
    tail[...] = jnp.zeros_like(tail)
    love_rows[...] = jnp.zeros_like(love_rows)
    love_rows[1:9, :] = love[...]
    love16 = love_rows[...]
    lane_row = lax.broadcasted_iota(jnp.int32, (128, 128), 0).astype(F32)
    step_f = step_in_tile.astype(F32)
    tile_row = lax.broadcasted_iota(jnp.int32, (8, 128), 0)

    def shifted_love(start):
        whole = jnp.floor(start * (1.0 / 128.0))
        picked = jnp.where(lane_row == start - 128.0 * whole, 1.0, 0.0).astype(F32)
        rows = jnp.dot(love16, picked, preferred_element_type=F32, precision=lax.Precision.HIGHEST)
        for bit in (4, 2, 1):
            half = jnp.floor(whole * (1.0 / bit))
            odd = half - 2.0 * jnp.floor(half * 0.5)
            rows = jnp.where(odd > 0.5, pltpu.roll(rows, 16 - bit, 0), rows)
        return rows

    def column_ids(t0):
        return 128 * tile_row + (16 * t0 + step_in_tile)

    pair_int = pair_lane.astype(jnp.int32)
    for t0 in range(8):
        low_love = shifted_love(step_f + (pair_lane + (16.0 * t0 + 128.0)))
        high_love = shifted_love(step_f + (16.0 * t0 + 127.0))
        is_low = column_ids(t0) < DEGREES - pair_int
        factor[8 * t0:8 * t0 + 8, :] = jnp.where(is_low, low_love[0:8], high_love[0:8])
        if t0 == 0:
            factor[64:72, :] = high_love[8:16]

    arrive(copies_pz)
    gathered = rp1[0]
    for i in range(1, 8):
        gathered = jnp.where(tile_row == i, rp1[i], gathered)
    mine = pl.ds(pl.multiple_of(8 * q, 8), 8)
    rp2[mine, :] = gathered
    copies_pq = send(FAR_FIRST, q, 8, q_device, lambda to: rp2.at[mine], lambda d: rp2.at[mine], sem_pq)
    arrive(copies_pq)
    wanted = perm[0:1, :]
    diagonal = tile_row == lane

    def onehot_rows(i, carry):
        pieces = []
        for half in range(2):
            row = rp2[pl.ds(2 * i + half, 1), :]
            column = jnp.sum(jnp.where(diagonal, jnp.broadcast_to(row, (8, 128)), 0.0), axis=1, keepdims=True)
            pieces.append(jnp.where(column == wanted, 1.0, 0.0))
        onehot[pl.ds(pl.multiple_of(16 * i, 16), 16), :] = jnp.concatenate(pieces, axis=0).astype(BF16)
        return carry

    lax.fori_loop(0, 32, onehot_rows, 0)

    table_copy.wait()
    arrive(copies1)
    f = [r1[i] for i in range(8)]
    a = [f[i] - f[i + 4] for i in range(4)]
    b = [f[i] + f[i + 4] for i in range(4)]
    root = math.sqrt(0.5)
    a13m = root * (a[1] - a[3])
    a13p = root * (a[1] + a[3])
    parts = (
        (b[0] + b[1] + b[2] + b[3], b[0] - b[1] + b[2] - b[3]),
        (a[0] + a13m, -a[2] - a13p),
        (b[0] - b[2], b[3] - b[1]),
        (a[0] - a13m, a[2] - a13p),
    )

    def turned(value, by):
        return pltpu.roll(value, by % 128, value.ndim - 1) if by % 128 else value

    for g in range(4):
        re, im = parts[g]
        for c in range(4):
            rhs[g, 40 * c:40 * c + 40, :] = jnp.where(
                quarter < 2,
                jnp.where(quarter == 0, turned(re, -32 * c), turned(im, 32 - 32 * c)),
                jnp.where(quarter == 2, turned(re, 64 - 32 * c), turned(im, 96 - 32 * c)),
            )
    for g in range(4):
        value = rhs[g]
        head = value.astype(BF16).astype(F32)
        both = jnp.where(lane < 64, head, value - head).astype(BF16)
        first = jnp.dot(table[g, 0], both, preferred_element_type=F32)
        second = jnp.dot(table[g, 1], both, preferred_element_type=F32)
        total = first + turned(first, 64) + second
        d1, d2 = total[0:256], total[256:512]
        if g:
            spectrum = d1 + jnp.where(quarter == 0, turned(d2, 96), -turned(d2, 32))
            flipped = jnp.where(quarter == 1, -spectrum, spectrum)
            rows = (spectrum[0:64], flipped[64:128], spectrum[128:192], flipped[192:256])
        else:
            plain = jnp.where(quarter == 0, d1, -turned(d2, 32))
            other = jnp.where(quarter == 0, turned(d1, 96), -d2)
            rows = (plain[0:64], other[64:128], plain[128:192], other[192:256])
        for half in range(2):
            at = 128 * g + 64 * half
            orders_all[at:at + 64, :] = jnp.where(lane < 64, rows[half], 0.0)
            orders_all[512 + at:512 + at + 64, :] = jnp.where(lane < 64, 0.0, turned(rows[2 + half], 64))
    value = orders_all[...]
    head = value.astype(BF16)
    rest = (value - head.astype(F32)).astype(BF16)
    in_slots = jnp.dot(onehot[...], head, preferred_element_type=F32) + jnp.dot(
        onehot[...], rest, preferred_element_type=F32
    )
    s2[...] = in_slots.reshape(8, 64, 128)
    copies2 = send(FAR_FIRST, q, 8, q_device, lambda to: s2.at[to], lambda d: r2.at[d], sem2)
    arrive(copies2)
    total = s2[q]
    for d in range(1, 8):
        total = total + r2[d]

    s3[...] = total.reshape(8, 8, 128)
    copies3 = send(FAR_FIRST, z, 8, z_device, lambda to: s3.at[to], lambda d: r3.at[z], sem3)
    r3[z] = s3[z]
    leg_copy.wait()
    tail[0:8, :] = leg[8192:8200, :].astype(F32)
    arrive(copies3)
    for r in range(2):
        for o in range(2):
            j = 2 * o + r
            for h in range(2):
                cols = slice(128 * h, 128 * h + 128)
                tile = turned(r3[4 * h], -32 * j)
                for g in range(1, 4):
                    tile = jnp.where(quarter == g, turned(r3[4 * h + g], 32 * (g - j)), tile)
                at = 16 * r + 8 * o
                four[at:at + 8, cols] = tile / float(TOTAL_LON) * quad[0:1, cols]
    fourier = four[...].astype(BF16)

    own_slot = lane % 8 == tile_row
    low_limit = DEGREES - pair_int - step_in_tile
    tail_rows = tail[...].astype(BF16)

    def row_of(t):
        return (t % 8) * 8 + t // 8

    for base in range(0, 64, 8):
        product = lax.dot_general(
            fourier, leg[128 * base:128 * base + 1024, :], (((1,), (1,)), ((), ())), preferred_element_type=F32
        )
        for t in range(base, base + 8):
            piece = product[:, 128 * (t - base):128 * (t - base) + 128]
            is_low = jnp.broadcast_to(16 * t < low_limit, (8, 128))
            chunk, row = divmod(row_of(t), 16)
            for r in range(2):
                picked = jnp.where(is_low, piece[16 * r:16 * r + 8], piece[16 * r + 8:16 * r + 16])
                summed = jnp.sum(jnp.where(own_slot, picked, 0.0), axis=0, keepdims=True)
                s4[chunk, 16 * r + row:16 * r + row + 1, :] = summed
    product = lax.dot_general(fourier, tail_rows, (((1,), (1,)), ((), ())), preferred_element_type=F32)
    for r in range(2):
        summed = jnp.sum(jnp.where(own_slot, product[16 * r + 8:16 * r + 16], 0.0), axis=0, keepdims=True)
        for chunk in range(4):
            s4[chunk, 32 + r:33 + r, :] = summed

    copies4 = send((2, 1, 3), x, 4, x_device, lambda to: s4.at[to], lambda d: r4.at[d], sem4)
    arrive(copies4)
    total = s4[x] + r4[1] + r4[2] + r4[3]
    own_factor = factor[pl.ds(pl.multiple_of(16 * x, 16), 16), :]
    scaled = jnp.concatenate([total[0:16] * own_factor, total[16:32] * own_factor], axis=0)
    r5[x] = scaled.astype(BF16)
    copies5 = send((2, 1, 3), x, 4, x_device, lambda to: r5.at[x], lambda d: r5.at[x], sem5)
    last_scaled = (total[32:40] * factor[64:65, :]).astype(BF16).astype(F32)
    arrive(copies5)

    for chunk in range(4):
        spectral = r5[chunk].astype(F32)
        for row in range(16):
            t0, t1 = divmod(16 * chunk + row, 8)
            t = 8 * t1 + t0
            is_low = jnp.broadcast_to(16 * t < low_limit, (8, 128))
            pieces = []
            for r in range(2):
                line = jnp.broadcast_to(spectral[16 * r + row:16 * r + row + 1], (8, 128))
                line = jnp.where(own_slot, line, 0.0)
                pieces += [jnp.where(is_low, line, 0.0), jnp.where(is_low, 0.0, line)]
            blocks[:, 128 * t:128 * t + 128] = jnp.concatenate(pieces, axis=0).astype(BF16)
    pieces = []
    for r in range(2):
        line = jnp.where(own_slot, jnp.broadcast_to(last_scaled[r:r + 1], (8, 128)), 0.0)
        pieces += [jnp.zeros((8, 128), F32), line]
    profile = jnp.dot(jnp.concatenate(pieces, axis=0).astype(BF16), tail_rows, preferred_element_type=F32)
    for base in range(0, 8192, 1024):
        profile = profile + jnp.dot(
            blocks[:, base:base + 1024], leg[base:base + 1024, :], preferred_element_type=F32
        )
    profile = profile.astype(BF16).astype(F32)

    for h in range(2):
        for g in range(4):
            tile = turned(profile[0:8, 128 * h:128 * h + 128], -32 * g)
            for j in range(1, 4):
                at = 16 * (j % 2) + 8 * (j // 2)
                tile = jnp.where(
                    quarter == j, turned(profile[at:at + 8, 128 * h:128 * h + 128], 32 * (j - g)), tile
                )
            s6[4 * h + g] = tile
    copies6 = send(FAR_FIRST, z, 8, z_device, lambda to: s6.at[to], lambda d: r6.at[z], sem6)
    r6[z] = s6[z]
    arrive(copies6)

    r7[q] = r6[...].reshape(64, 128).astype(BF16)
    copies7 = send(FAR_FIRST, q, 8, q_device, lambda to: r7.at[q], lambda d: r7.at[q], sem7)
    arrive(copies7)
    natural = lax.dot_general(
        r7[...].reshape(512, 128), onehot[...], (((0,), (0,)), ((), ())), preferred_element_type=F32
    )
    wide_lane = lax.broadcasted_iota(jnp.int32, (1, 256), 1)
    second_half = wide_lane % 128 >= 64
    waves = []
    for g in range(4):
        low = slice(128 * g, 128 * g + 128)
        high = slice(512 + 128 * g, 640 + 128 * g)
        re = jnp.concatenate([natural[0:32, low], natural[64:96, high]], axis=1)
        im = jnp.concatenate([natural[32:64, low], natural[96:128, high]], axis=1)
        if g:
            left = jnp.concatenate([re, jnp.where(second_half, -im, im)], axis=0)
        else:
            re = jnp.where(wide_lane == 0, 0.5 * re, re)
            im = jnp.where(wide_lane == 0, 0.5 * im, im)
            left = jnp.concatenate([
                jnp.where(second_half, 0.0, re), jnp.where(second_half, 0.0, im),
                jnp.where(second_half, re, 0.0), jnp.where(second_half, im, 0.0),
            ], axis=0)
        left = left.astype(BF16)
        by_cos = jnp.dot(left, table[g, 0, 0:256], preferred_element_type=F32) + jnp.dot(
            left, table[g, 1, 0:256], preferred_element_type=F32
        )
        by_sin = jnp.dot(left, table[g, 0, 256:512], preferred_element_type=F32) + jnp.dot(
            left, table[g, 1, 256:512], preferred_element_type=F32
        )
        if g:
            waves.append((by_cos[0:32] - by_sin[32:64], by_sin[0:32] + by_cos[32:64]))
        else:
            waves.append((by_cos[0:32] - by_sin[32:64], by_cos[64:96] - by_sin[96:128]))
    (w0, w4), (re1, im1), (re2, im2), (re3, im3) = waves
    even0, even1 = w0 + w4, w0 - w4
    re_sum, re_dif = re1 + re3, root * (re1 - re3)
    im_dif, im_sum = im1 - im3, root * (im1 + im3)
    b0, b1, b2, b3 = even0 + re2, even1 - im2, even0 - re2, even1 + im2
    a0, a1, a2, a3 = re_sum, re_dif - im_sum, -im_dif, -re_dif - im_sum
    for i, value in enumerate((b0 + a0, b1 + a1, b2 + a2, b3 + a3, b0 - a0, b1 - a1, b2 - a2, b3 - a3)):
        s8[i] = (2.0 * value).astype(BF16)

    copies8 = send(FAR_FIRST, z, 8, z_device, lambda to: s8.at[to], lambda d: r8.at[z], sem8)
    r8[z] = s8[z]
    arrive(copies8)
    grid = r8[...].reshape(256, 256).astype(F32).T
    out[...] = grid[0:135, :]
    for copy in started:
        copy.wait_send()


def per_device(field, quad_weight, legendre, love_factor, pair_table):
    low, high = pair_orders()
    perm = np.broadcast_to(np.concatenate([low, high]).astype(np.float32), (8, 1024))
    pair_rows = jnp.broadcast_to(jnp.tile(pair_table.astype(F32), 16), (8, 128))
    vmem = pl.BlockSpec(memory_space=pltpu.VMEM)
    anywhere = pl.BlockSpec(memory_space=pl.ANY)
    pair_sems = pltpu.SemaphoreType.DMA((2, 8))
    grid = pl.pallas_call(
        kernel,
        out_shape=jax.ShapeDtypeStruct((LON_COLS, 256), F32),
        in_specs=[vmem] * 5 + [anywhere] * 2,
        out_specs=vmem,
        scratch_shapes=[
            pltpu.VMEM((8200, 256), BF16),
            pltpu.VMEM((4, 2, 512, 256), BF16),
            pltpu.VMEM((128, 256), F32),
            pltpu.VMEM((40, 256), F32),
            pltpu.VMEM((8, 40, 128), F32),
            pltpu.VMEM((8, 40, 128), F32),
            pltpu.VMEM((8, 8, 128), F32),
            pltpu.VMEM((64, 128), F32),
            pltpu.VMEM((512, 1024), BF16),
            pltpu.VMEM((4, 256, 128), F32),
            pltpu.VMEM((1024, 128), F32),
            pltpu.VMEM((8, 64, 128), F32),
            pltpu.VMEM((8, 64, 128), F32),
            pltpu.VMEM((8, 8, 128), F32),
            pltpu.VMEM((8, 8, 128), F32),
            pltpu.VMEM((32, 256), F32),
            pltpu.VMEM((4, 40, 128), F32),
            pltpu.VMEM((4, 40, 128), F32),
            pltpu.VMEM((4, 32, 128), BF16),
            pltpu.VMEM((72, 128), F32),
            pltpu.VMEM((16, 128), F32),
            pltpu.VMEM((32, 8192), BF16),
            pltpu.VMEM((8, 8, 128), F32),
            pltpu.VMEM((8, 8, 128), F32),
            pltpu.VMEM((8, 64, 128), BF16),
            pltpu.VMEM((8, 32, 256), BF16),
            pltpu.VMEM((8, 32, 256), BF16),
            pltpu.SemaphoreType.DMA((2,)),
        ] + [pair_sems] * 10,
        compiler_params=pltpu.CompilerParams(
            collective_id=0, has_side_effects=True, vmem_limit_bytes=40 * 1024 * 1024
        ),
    )(
        field.T,
        quad_weight.reshape(1, 256),
        love_factor.reshape(8, 128),
        pair_rows,
        jnp.asarray(perm),
        legendre.transpose(1, 0, 2).reshape(8200, 256),
        jnp.asarray(angle_constants()),
    )
    return grid.T


def solution(mesh):
    placed = (P("lat", "lon"), P("lat"), P("lon", None, "lat"), P(), P("lon"))
    return jax.shard_map(
        per_device, mesh=mesh, in_specs=placed, out_specs=P("lat", "lon"), check_vma=False
    )
```

time: 328 us -> 65.3 us (0.20)
  waiting for transfers between devices: 248 us -> 0 us
  Pallas kernels: 0 us -> 58.5 us
  matrix products: 21.2 us -> 0 us
  blocking collectives: 20.7 us -> 0 us
  between operations: 13.9 us -> 0.02 us
  local copies, waits for them, and re-layouts: 19.2 us -> 5.91 us
  other arithmetic: 4.23 us -> 0.66 us
    reduce_scatter x1 -> x0, waiting for transfers between devices: 121 us -> none  [per_device(): lax.psum_scatter(stacked / total_lon, 'lon', scatter_dimension=0, tiled=T...]
    all_gather x1 -> x0, waiting for transfers between devices: 79.8 us -> none  [per_device(): shard_piece = lax.all_gather(order_fields, 'lon', axis=0, tiled=True)]
    pallas_call x0 -> x1, Pallas kernels: none -> 58.5 us  [per_device(): pl.pallas_call(kernel, out_shape=jax.ShapeDtypeStruct((LON_COLS, 256), F3...]
    psum x1 -> x0, waiting for transfers between devices: 46.7 us -> none  [per_device(): coefficient = lax.psum(coefficient, 'lat')]
    dot_general x6 -> x0, matrix products: 21.2 us -> none  [the longest x1 3.82 us: per_device(): jnp.einsum('spb,lb->spl', sin_table, field, precision=lax.Precision.HIGHEST)]
    unnamed x1 -> x0, blocking collectives: 20.7 us -> none
    gather x32 -> x0, local copies, waits for them, and re-layouts: 12 us -> none
  transfers between devices with their start and end apart: 3 -> 0, of which waited for: 3 -> 0; matrix products, arithmetic and copies ran while one was open for 4% -> 0% of each run, Pallas kernels for 0% -> 0%
where the time goes in v1:
time: 65.3 us; the launch traced here: 65.1 us
  Pallas kernels  58.5 us (90%)
  local copies, waits for them, and re-layouts  5.91 us (9%)
  other arithmetic  0.66 us (1%)
    pallas_call x1, Pallas kernels, per_device(): pl.pallas_call(kernel, out_shape=jax.ShapeDtypeStruct((LON_COLS, 256), F3...  58.5 us
    unnamed x9, local copies, waits for them, and re-layouts  5.12 us

profile of v1, /device:TPU:1, one launch (start us, length us, event | category | flops | bytes accessed | tf_op | source)
XLA Modules:
  0.0 65.1 jit_solution(4970900969903579923)
XLA Ops:
  0.0 0.7 %convert_element_type.3 = f32[8]{0:T(128)S(1)} convert(s32[8]{0:T(128)} %param.11) | non-fusion elementwise | flops 8 | bytes 64 | tf_op jit(solution)/shard_map/convert_element_type | solution.py:381
  0.7 0.1 tile.10
  0.8 0.7 %jit_solution_.3.perm = f32[8,1024]{1,0:T(8,128)S(1)} broadcast(f32[1024]{0:T(1024)} %constant.4.clone), dimensions={1} | broadcast | bytes 36864 | tf_op jit(solution)
  1.5 0.0 copy-start
  1.5 2.2 %copy-done = bf16[8,1025,256]{2,0,1:T(8,128)(2,1)S(1)} copy-done((bf16[8,1025,256]{2,0,1:T(8,128)(2,1)S(1)}, bf16[8,1025,256]{2,0,1:T(8,128)(2,1)}, u32[]{:S(2)}) %copy-start) | copy-done | bytes 4198424
  3.6 0.0 copy-start.1
  3.6 0.9 %copy-done.1 = f32[256,135]{0,1:T(8,128)S(1)} copy-done((f32[256,135]{0,1:T(8,128)S(1)}, f32[256,135]{0,1:T(8,128)}, u32[]{:S(2)}) %copy-start.1) | copy-done | bytes 138264
  4.6 0.0 copy-start.2
  4.6 0.7 %copy-done.2 = f32[1024]{0:T(1024)S(1)} copy-done((f32[1024]{0:T(1024)S(1)}, f32[1024]{0:T(1024)}, u32[]{:S(2)}) %copy-start.2) | copy-done | bytes 4120
  5.2 0.0 copy-start.3
  5.2 0.7 %copy-done.3 = f32[256]{0:T(256)S(1)} copy-done((f32[256]{0:T(256)S(1)}, f32[256]{0:T(256)}, u32[]{:S(2)}) %copy-start.3) | copy-done | bytes 1048
  5.9 58.5 %shard_map.73 = f32[135,256]{1,0:T(8,128)S(1)} custom-call(f32[135,256]{1,0:T(8,128)S(1)} %bitcast.9, f32[1,256]{1,0:T(1,128)S(1)} %bitcast.11, f32[8,128]{1,0:T(8,128)S(1)} %bitcast.10, f32[8,128]{1,0:T(8,128)S(1)} %broadcast_in_dim.3.pairs, f32[8,1024]{1,0:T(8,128)S(1)} %jit_solution_.3.perm, bf16[8200,256]{1,0:T(8,128)(2,1)S(1)} %bitcast.7, ...), custom_call_target="tpu_custom_call" | custom-call | tf_op jit(solution)/shard_map/pallas_call | solution.py:385
  64.5 0.7 %copy.9 = f32[256,135]{0,1:T(8,128)} copy(f32[256,135]{0,1:T(8,128)S(1)} %bitcast.8) | data formatting | bytes 276480
  (2 shorter events, 0.0 us)
Async XLA Ops:
  1.5 2.2 %copy-start = (bf16[8,1025,256]{2,0,1:T(8,128)(2,1)S(1)}, bf16[8,1025,256]{2,0,1:T(8,128)(2,1)}, u32[]{:S(2)}) copy-start(bf16[8,1025,256]{2,0,1:T(8,128)(2,1)} %param.9) | copy-start | bytes 12595204
  3.6 0.9 %copy-start.1 = (f32[256,135]{0,1:T(8,128)S(1)}, f32[256,135]{0,1:T(8,128)}, u32[]{:S(2)}) copy-start(f32[256,135]{0,1:T(8,128)} %param.7) | copy-start | bytes 414724
  4.6 0.7 %copy-start.2 = (f32[1024]{0:T(1024)S(1)}, f32[1024]{0:T(1024)}, u32[]{:S(2)}) copy-start(f32[1024]{0:T(1024)} %param.10) | copy-start | bytes 12292
  5.2 0.7 %copy-start.3 = (f32[256]{0:T(256)S(1)}, f32[256]{0:T(256)}, u32[]{:S(2)}) copy-start(f32[256]{0:T(256)} %param.8) | copy-start | bytes 3076

commit v2 on v1

--- a/solution.py
+++ b/solution.py
@@ -47,8 +47,8 @@
 
 
 def kernel(
-    field, quad, love, pairs, perm, legendre, angles, out,
-    leg, table, tail, last_rows, s1, r1, rp1, rp2, onehot, rhs, orders_all, s2, r2, s3, r3, four, s4, r4, r5,
+    field_in, quad_in, love_in, pair_in, legendre, angles, out,
+    field, quad, love, pair_own, pairs, leg, table, tail, last_rows, s1, r1, rp1, rp2, onehot, rhs, orders_all, s2, r2, s3, r3, four, s4, r4, r5,
     factor, love_rows, blocks, s6, r6, r7, s8, r8,
     local_sem, sem_pz, sem_pq, sem1, sem2, sem3, sem4, sem5, sem6, sem7, sem8,
 ):
@@ -73,10 +73,14 @@
     for d in range(1, 4):
         pl.semaphore_signal(barrier, inc=1, device_id=x_device((x + d) % 4))
 
+    field_copy = pltpu.make_async_copy(field_in, field, local_sem.at[2])
+    pair_copy = pltpu.make_async_copy(pair_in, pair_own, local_sem.at[3])
+    love_copy = pltpu.make_async_copy(love_in, love, local_sem.at[4])
+    quad_copy = pltpu.make_async_copy(quad_in, quad, local_sem.at[5])
     leg_copy = pltpu.make_async_copy(legendre, leg, local_sem.at[0])
     table_copy = pltpu.make_async_copy(angles.at[q], table, local_sem.at[1])
-    leg_copy.start()
-    table_copy.start()
+    for copy in (pair_copy, field_copy, love_copy, quad_copy, table_copy, leg_copy):
+        copy.start()
 
     started = []
 
@@ -85,7 +89,7 @@
         for d in distances:
             to = (me + d) % size
             copy = pltpu.make_async_remote_copy(
-                src_ref=source(to), dst_ref=target(d),
+                src_ref=source(to, d), dst_ref=target(d),
                 send_sem=sems.at[0, d], recv_sem=sems.at[1, d],
                 device_id=device(to),
             )
@@ -103,6 +107,12 @@
     step_in_tile = lane // 8
 
     last_rows[...] = jnp.zeros_like(last_rows)
+    pair_copy.wait()
+    spread = jnp.concatenate([pair_own[...].astype(F32), jnp.zeros((1, 120), F32)], axis=1)
+    for shift in (8, 16, 32, 64):
+        spread = spread + pltpu.roll(spread, shift, 1)
+    pairs[...] = jnp.broadcast_to(spread, (8, 128))
+    field_copy.wait()
     last_rows[0:15, :] = field[120:135, :]
     for h in range(2):
         cols = slice(128 * h, 128 * h + 128)
@@ -115,21 +125,30 @@
             s1[4 * h + g] = packed
 
     pl.semaphore_wait(barrier, 17)
-    copies_pz = send(FAR_FIRST, z, 8, z_device, lambda to: pairs, lambda d: rp1.at[z], sem_pz)
-    copies1 = send(FAR_FIRST, z, 8, z_device, lambda to: s1.at[to], lambda d: r1.at[z], sem1)
+    copies_pz = send(FAR_FIRST, z, 8, z_device, lambda to, d: pairs, lambda d: rp1.at[z], sem_pz)
+    copies1 = send(FAR_FIRST, z, 8, z_device, lambda to, d: s1.at[to], lambda d: r1.at[z], sem1)
     r1[z] = s1[z]
     rp1[z] = pairs[...]
 
-    pair_lane = pairs[0:1, :]
+    tile_row = lax.broadcasted_iota(jnp.int32, (8, 128), 0)
     rhs[...] = jnp.zeros_like(rhs)
     s4[...] = jnp.zeros_like(s4)
     tail[...] = jnp.zeros_like(tail)
     love_rows[...] = jnp.zeros_like(love_rows)
+    arrive(copies_pz)
+    gathered = rp1[0]
+    for i in range(1, 8):
+        gathered = jnp.where(tile_row == i, rp1[i], gathered)
+    mine = pl.ds(pl.multiple_of(8 * q, 8), 8)
+    rp2[mine, :] = gathered
+    copies_pq = send(FAR_FIRST, q, 8, q_device, lambda to, d: rp2.at[mine], lambda d: rp2.at[mine], sem_pq)
+
+    pair_lane = pairs[0:1, :]
+    love_copy.wait()
     love_rows[1:9, :] = love[...]
     love16 = love_rows[...]
     lane_row = lax.broadcasted_iota(jnp.int32, (128, 128), 0).astype(F32)
     step_f = step_in_tile.astype(F32)
-    tile_row = lax.broadcasted_iota(jnp.int32, (8, 128), 0)
 
     def shifted_love(start):
         whole = jnp.floor(start * (1.0 / 128.0))
@@ -149,31 +168,20 @@
         low_love = shifted_love(step_f + (pair_lane + (16.0 * t0 + 128.0)))
         high_love = shifted_love(step_f + (16.0 * t0 + 127.0))
         is_low = column_ids(t0) < DEGREES - pair_int
-        factor[8 * t0:8 * t0 + 8, :] = jnp.where(is_low, low_love[0:8], high_love[0:8])
+        factor[pl.ds(t0, 8, stride=8), :] = jnp.where(is_low, low_love[0:8], high_love[0:8])
         if t0 == 0:
             factor[64:72, :] = high_love[8:16]
 
-    arrive(copies_pz)
-    gathered = rp1[0]
-    for i in range(1, 8):
-        gathered = jnp.where(tile_row == i, rp1[i], gathered)
-    mine = pl.ds(pl.multiple_of(8 * q, 8), 8)
-    rp2[mine, :] = gathered
-    copies_pq = send(FAR_FIRST, q, 8, q_device, lambda to: rp2.at[mine], lambda d: rp2.at[mine], sem_pq)
+    place = lax.broadcasted_iota(jnp.int32, (1, 1024), 1)
+    group = place % 512 // 128
+    other = jnp.where(group == 0, 4, 8 - group)
+    residue = jnp.where(place % 128 < 64, group, other)
+    wanted = (8 * (place % 64) + jnp.where(place < 512, residue, 7 - residue)).astype(F32)
     arrive(copies_pq)
-    wanted = perm[0:1, :]
-    diagonal = tile_row == lane
-
-    def onehot_rows(i, carry):
-        pieces = []
-        for half in range(2):
-            row = rp2[pl.ds(2 * i + half, 1), :]
-            column = jnp.sum(jnp.where(diagonal, jnp.broadcast_to(row, (8, 128)), 0.0), axis=1, keepdims=True)
-            pieces.append(jnp.where(column == wanted, 1.0, 0.0))
-        onehot[pl.ds(pl.multiple_of(16 * i, 16), 16), :] = jnp.concatenate(pieces, axis=0).astype(BF16)
-        return carry
-
-    lax.fori_loop(0, 32, onehot_rows, 0)
+    spread = jnp.broadcast_to(rp2[...].reshape(64, 1, 128), (64, 8, 128))
+    diagonal = (tile_row == lane).reshape(1, 8, 128)
+    column = jnp.sum(jnp.where(diagonal, spread, 0.0), axis=2, keepdims=True).reshape(512, 1)
+    onehot[...] = jnp.where(column == wanted, 1.0, 0.0).astype(BF16)
 
     table_copy.wait()
     arrive(copies1)
@@ -224,19 +232,26 @@
     value = orders_all[...]
     head = value.astype(BF16)
     rest = (value - head.astype(F32)).astype(BF16)
-    in_slots = jnp.dot(onehot[...], head, preferred_element_type=F32) + jnp.dot(
-        onehot[...], rest, preferred_element_type=F32
-    )
-    s2[...] = in_slots.reshape(8, 64, 128)
-    copies2 = send(FAR_FIRST, q, 8, q_device, lambda to: s2.at[to], lambda d: r2.at[d], sem2)
+    copies2 = []
+    for part in ((4, 3, 5, 2), (6, 1, 7, 0)):
+        rows = jnp.concatenate(
+            [onehot[pl.ds(pl.multiple_of((q + d) % 8 * 64, 64), 64), :] for d in part], axis=0
+        )
+        in_slots = jnp.dot(rows, head, preferred_element_type=F32) + jnp.dot(rows, rest, preferred_element_type=F32)
+        for i, d in enumerate(part):
+            s2[d] = in_slots[64 * i:64 * i + 64]
+        copies2 += send(
+            [d for d in part if d], q, 8, q_device, lambda to, d: s2.at[d], lambda d: r2.at[d], sem2
+        )
     arrive(copies2)
-    total = s2[q]
+    total = s2[0]
     for d in range(1, 8):
         total = total + r2[d]
 
     s3[...] = total.reshape(8, 8, 128)
-    copies3 = send(FAR_FIRST, z, 8, z_device, lambda to: s3.at[to], lambda d: r3.at[z], sem3)
+    copies3 = send(FAR_FIRST, z, 8, z_device, lambda to, d: s3.at[to], lambda d: r3.at[z], sem3)
     r3[z] = s3[z]
+    quad_copy.wait()
     leg_copy.wait()
     tail[0:8, :] = leg[8192:8200, :].astype(F32)
     arrive(copies3)
@@ -256,58 +271,61 @@
     low_limit = DEGREES - pair_int - step_in_tile
     tail_rows = tail[...].astype(BF16)
 
-    def row_of(t):
-        return (t % 8) * 8 + t // 8
-
-    for base in range(0, 64, 8):
-        product = lax.dot_general(
-            fourier, leg[128 * base:128 * base + 1024, :], (((1,), (1,)), ((), ())), preferred_element_type=F32
-        )
-        for t in range(base, base + 8):
-            piece = product[:, 128 * (t - base):128 * (t - base) + 128]
-            is_low = jnp.broadcast_to(16 * t < low_limit, (8, 128))
-            chunk, row = divmod(row_of(t), 16)
-            for r in range(2):
-                picked = jnp.where(is_low, piece[16 * r:16 * r + 8], piece[16 * r + 8:16 * r + 16])
-                summed = jnp.sum(jnp.where(own_slot, picked, 0.0), axis=0, keepdims=True)
-                s4[chunk, 16 * r + row:16 * r + row + 1, :] = summed
+    def analysed(piece, is_low, r):
+        if is_low is None:
+            picked = piece[16 * r + 8:16 * r + 16]
+        else:
+            picked = jnp.where(is_low, piece[16 * r:16 * r + 8], piece[16 * r + 8:16 * r + 16])
+        return jnp.sum(jnp.where(own_slot, picked, 0.0), axis=0, keepdims=True)
+
+    def chunk_rows(chunk):
+        return pl.ds(pl.multiple_of(2048 * chunk, 2048), 2048)
+
     product = lax.dot_general(fourier, tail_rows, (((1,), (1,)), ((), ())), preferred_element_type=F32)
     for r in range(2):
-        summed = jnp.sum(jnp.where(own_slot, product[16 * r + 8:16 * r + 16], 0.0), axis=0, keepdims=True)
-        for chunk in range(4):
-            s4[chunk, 32 + r:33 + r, :] = summed
-
-    copies4 = send((2, 1, 3), x, 4, x_device, lambda to: s4.at[to], lambda d: r4.at[d], sem4)
+        summed = analysed(product, None, r)
+        for d in range(4):
+            s4[d, 32 + r:33 + r, :] = summed
+    copies4 = []
+    for d in (2, 1, 3, 0):
+        chunk = (x + d) % 4
+        product = lax.dot_general(
+            fourier, leg[chunk_rows(chunk), :], (((1,), (1,)), ((), ())), preferred_element_type=F32
+        )
+        for row in range(16):
+            is_low = jnp.broadcast_to(16 * (16 * chunk + row) < low_limit, (8, 128))
+            for r in range(2):
+                s4[d, 16 * r + row:16 * r + row + 1, :] = analysed(product[:, 128 * row:128 * row + 128], is_low, r)
+        if d:
+            copies4 += send((d,), x, 4, x_device, lambda to, d: s4.at[d], lambda d: r4.at[d], sem4)
+
     arrive(copies4)
-    total = s4[x] + r4[1] + r4[2] + r4[3]
+    total = s4[0] + r4[1] + r4[2] + r4[3]
     own_factor = factor[pl.ds(pl.multiple_of(16 * x, 16), 16), :]
     scaled = jnp.concatenate([total[0:16] * own_factor, total[16:32] * own_factor], axis=0)
-    r5[x] = scaled.astype(BF16)
-    copies5 = send((2, 1, 3), x, 4, x_device, lambda to: r5.at[x], lambda d: r5.at[x], sem5)
+    r5[0] = scaled.astype(BF16)
+    copies5 = send((2, 1, 3), x, 4, x_device, lambda to, d: r5.at[0], lambda d: r5.at[d], sem5)
     last_scaled = (total[32:40] * factor[64:65, :]).astype(BF16).astype(F32)
-    arrive(copies5)
-
-    for chunk in range(4):
-        spectral = r5[chunk].astype(F32)
+
+    pieces = []
+    for r in range(2):
+        line = jnp.where(own_slot, jnp.broadcast_to(last_scaled[r:r + 1], (8, 128)), 0.0)
+        pieces += [jnp.zeros((8, 128), F32), line]
+    profile = jnp.dot(jnp.concatenate(pieces, axis=0).astype(BF16), tail_rows, preferred_element_type=F32)
+    for d in (0, 1, 3, 2):
+        if d:
+            arrive([copies5[(2, 1, 3).index(d)]])
+        chunk = (x - d + 4) % 4
+        spectral = r5[d].astype(F32)
         for row in range(16):
-            t0, t1 = divmod(16 * chunk + row, 8)
-            t = 8 * t1 + t0
-            is_low = jnp.broadcast_to(16 * t < low_limit, (8, 128))
+            is_low = jnp.broadcast_to(16 * (16 * chunk + row) < low_limit, (8, 128))
             pieces = []
             for r in range(2):
                 line = jnp.broadcast_to(spectral[16 * r + row:16 * r + row + 1], (8, 128))
                 line = jnp.where(own_slot, line, 0.0)
                 pieces += [jnp.where(is_low, line, 0.0), jnp.where(is_low, 0.0, line)]
-            blocks[:, 128 * t:128 * t + 128] = jnp.concatenate(pieces, axis=0).astype(BF16)
-    pieces = []
-    for r in range(2):
-        line = jnp.where(own_slot, jnp.broadcast_to(last_scaled[r:r + 1], (8, 128)), 0.0)
-        pieces += [jnp.zeros((8, 128), F32), line]
-    profile = jnp.dot(jnp.concatenate(pieces, axis=0).astype(BF16), tail_rows, preferred_element_type=F32)
-    for base in range(0, 8192, 1024):
-        profile = profile + jnp.dot(
-            blocks[:, base:base + 1024], leg[base:base + 1024, :], preferred_element_type=F32
-        )
+            blocks[d, :, 128 * row:128 * row + 128] = jnp.concatenate(pieces, axis=0).astype(BF16)
+        profile = profile + jnp.dot(blocks[d], leg[chunk_rows(chunk), :], preferred_element_type=F32)
     profile = profile.astype(BF16).astype(F32)
 
     for h in range(2):
@@ -319,12 +337,12 @@
                     quarter == j, turned(profile[at:at + 8, 128 * h:128 * h + 128], 32 * (j - g)), tile
                 )
             s6[4 * h + g] = tile
-    copies6 = send(FAR_FIRST, z, 8, z_device, lambda to: s6.at[to], lambda d: r6.at[z], sem6)
+    copies6 = send(FAR_FIRST, z, 8, z_device, lambda to, d: s6.at[to], lambda d: r6.at[z], sem6)
     r6[z] = s6[z]
     arrive(copies6)
 
     r7[q] = r6[...].reshape(64, 128).astype(BF16)
-    copies7 = send(FAR_FIRST, q, 8, q_device, lambda to: r7.at[q], lambda d: r7.at[q], sem7)
+    copies7 = send(FAR_FIRST, q, 8, q_device, lambda to, d: r7.at[q], lambda d: r7.at[q], sem7)
     arrive(copies7)
     natural = lax.dot_general(
         r7[...].reshape(512, 128), onehot[...], (((0,), (0,)), ((), ())), preferred_element_type=F32
@@ -366,7 +384,7 @@
     for i, value in enumerate((b0 + a0, b1 + a1, b2 + a2, b3 + a3, b0 - a0, b1 - a1, b2 - a2, b3 - a3)):
         s8[i] = (2.0 * value).astype(BF16)
 
-    copies8 = send(FAR_FIRST, z, 8, z_device, lambda to: s8.at[to], lambda d: r8.at[z], sem8)
+    copies8 = send(FAR_FIRST, z, 8, z_device, lambda to, d: s8.at[to], lambda d: r8.at[z], sem8)
     r8[z] = s8[z]
     arrive(copies8)
     grid = r8[...].reshape(256, 256).astype(F32).T
@@ -376,18 +394,20 @@
 
 
 def per_device(field, quad_weight, legendre, love_factor, pair_table):
-    low, high = pair_orders()
-    perm = np.broadcast_to(np.concatenate([low, high]).astype(np.float32), (8, 1024))
-    pair_rows = jnp.broadcast_to(jnp.tile(pair_table.astype(F32), 16), (8, 128))
     vmem = pl.BlockSpec(memory_space=pltpu.VMEM)
     anywhere = pl.BlockSpec(memory_space=pl.ANY)
     pair_sems = pltpu.SemaphoreType.DMA((2, 8))
     grid = pl.pallas_call(
         kernel,
         out_shape=jax.ShapeDtypeStruct((LON_COLS, 256), F32),
-        in_specs=[vmem] * 5 + [anywhere] * 2,
+        in_specs=[anywhere] * 6,
         out_specs=vmem,
         scratch_shapes=[
+            pltpu.VMEM((LON_COLS, 256), F32),
+            pltpu.VMEM((1, 256), F32),
+            pltpu.VMEM((8, 128), F32),
+            pltpu.VMEM((1, 8), jnp.int32),
+            pltpu.VMEM((8, 128), F32),
             pltpu.VMEM((8200, 256), BF16),
             pltpu.VMEM((4, 2, 512, 256), BF16),
             pltpu.VMEM((128, 256), F32),
@@ -409,23 +429,22 @@
             pltpu.VMEM((4, 32, 128), BF16),
             pltpu.VMEM((72, 128), F32),
             pltpu.VMEM((16, 128), F32),
-            pltpu.VMEM((32, 8192), BF16),
+            pltpu.VMEM((4, 32, 2048), BF16),
             pltpu.VMEM((8, 8, 128), F32),
             pltpu.VMEM((8, 8, 128), F32),
             pltpu.VMEM((8, 64, 128), BF16),
             pltpu.VMEM((8, 32, 256), BF16),
             pltpu.VMEM((8, 32, 256), BF16),
-            pltpu.SemaphoreType.DMA((2,)),
+            pltpu.SemaphoreType.DMA((6,)),
         ] + [pair_sems] * 10,
         compiler_params=pltpu.CompilerParams(
-            collective_id=0, has_side_effects=True, vmem_limit_bytes=40 * 1024 * 1024
+            collective_id=0, has_side_effects=True, vmem_limit_bytes=60 * 1024 * 1024
         ),
     )(
         field.T,
         quad_weight.reshape(1, 256),
         love_factor.reshape(8, 128),
-        pair_rows,
-        jnp.asarray(perm),
+        pair_table.reshape(1, 8),
         legendre.transpose(1, 0, 2).reshape(8200, 256),
         jnp.asarray(angle_constants()),
     )

time: 65.3 us -> 56.2 us (0.86)
  local copies, waits for them, and re-layouts: 5.91 us -> 1.57 us
  Pallas kernels: 58.5 us -> 54.5 us
  other arithmetic: 0.66 us -> 0 us
    pallas_call x1, Pallas kernels: 58.5 us -> 54.5 us  [per_device(): pl.pallas_call(kernel, out_shape=jax.ShapeDtypeStruct((LON_COLS, 256), F3...]
    unnamed x9 -> x1, local copies, waits for them, and re-layouts: 5.12 us -> 1.57 us
    another operation x3 -> x0, local copies, waits for them, and re-layouts: 0.78 us -> none
    convert_element_type x1 -> x0, other arithmetic: 0.66 us -> none  [per_device(): pair_rows = jnp.broadcast_to(jnp.tile(pair_table.astype(F32), 16), (8, 128))]
where the time goes in v2:
time: 56.2 us; the launch traced here: 56.1 us
  Pallas kernels  54.5 us (97%)
  local copies, waits for them, and re-layouts  1.57 us (3%)
    pallas_call x1, Pallas kernels, per_device(): pl.pallas_call(kernel, out_shape=jax.ShapeDtypeStruct((LON_COLS, 256), F3...  54.5 us
    unnamed x1, local copies, waits for them, and re-layouts  1.57 us

profile of v2, /device:TPU:1, one launch (start us, length us, event | category | flops | bytes accessed | tf_op | source)
XLA Modules:
  0.0 56.1 jit_solution(8473426860865864953)
XLA Ops:
  0.0 54.5 %shard_map.64 = f32[135,256]{1,0:T(8,128)} custom-call(f32[135,256]{1,0:T(8,128)} %bitcast.10, f32[1,256]{1,0:T(1,128)} %bitcast.12, f32[8,128]{1,0:T(8,128)} %bitcast.11, s32[1,8]{1,0:T(1,128)} %bitcast.13, bf16[8200,256]{1,0:T(8,128)(2,1)} %bitcast.8, bf16[8,4,2,512,256]{4,3,2,1,0:T(8,128)(2,1)} %constant.2.clone.angles), custom_call_target="tpu_custom_call" | custom-call | tf_op jit(solution)/shard_map/pallas_call | solution.py:400
  54.6 1.6 %copy.8 = f32[256,135]{0,1:T(8,128)} copy(f32[256,135]{0,1:T(8,128)} %bitcast.9) | data formatting | bytes 276480

commit v3 on v2

--- a/solution.py
+++ b/solution.py
@@ -48,9 +48,9 @@
 
 def kernel(
     field_in, quad_in, love_in, pair_in, legendre, angles, out,
-    field, quad, love, pair_own, pairs, leg, table, tail, last_rows, s1, r1, rp1, rp2, onehot, rhs, orders_all, s2, r2, s3, r3, four, s4, r4, r5,
-    factor, love_rows, blocks, s6, r6, r7, s8, r8,
-    local_sem, sem_pz, sem_pq, sem1, sem2, sem3, sem4, sem5, sem6, sem7, sem8,
+    field, quad, love, pair_own, pairs, leg, table, tail, last_rows, s1, r1, rp1, rp2, onehot, rhs, orders_all, s2, r2, s3, r3, four, s4, r4,
+    factor, love_rows, blocks, s6, r6, r7, s8,
+    local_sem, sem_pz, sem_pq, sem1, sem2, sem3, sem6, sem7, sem8, sem4,
 ):
     lon = lax.axis_index("lon")
     x = lax.axis_index("lat")
@@ -67,8 +67,9 @@
         return {"lat": i}
 
     barrier = pltpu.get_barrier_semaphore()
-    for d in range(1, 8):
+    for d in FAR_FIRST:
         pl.semaphore_signal(barrier, inc=1, device_id=z_device((z + d) % 8))
+    for d in FAR_FIRST:
         pl.semaphore_signal(barrier, inc=1, device_id=q_device((q + d) % 8))
     for d in range(1, 4):
         pl.semaphore_signal(barrier, inc=1, device_id=x_device((x + d) % 4))
@@ -82,7 +83,7 @@
     for copy in (pair_copy, field_copy, love_copy, quad_copy, table_copy, leg_copy):
         copy.start()
 
-    started = []
+    unsettled = []
 
     def send(distances, me, size, device, source, target, sems):
         copies = []
@@ -95,8 +96,12 @@
             )
             copy.start()
             copies.append(copy)
-        started.extend(copies)
+        unsettled.extend(copies)
         return copies
+
+    def settle(keep=0):
+        while len(unsettled) > keep:
+            unsettled.pop(0).wait_send()
 
     def arrive(copies):
         for copy in copies:
@@ -125,23 +130,22 @@
             s1[4 * h + g] = packed
 
     pl.semaphore_wait(barrier, 17)
-    copies_pz = send(FAR_FIRST, z, 8, z_device, lambda to, d: pairs, lambda d: rp1.at[z], sem_pz)
+    copies_pq = send(FAR_FIRST, q, 8, q_device, lambda to, d: pairs, lambda d: rp1.at[q], sem_pq)
     copies1 = send(FAR_FIRST, z, 8, z_device, lambda to, d: s1.at[to], lambda d: r1.at[z], sem1)
     r1[z] = s1[z]
-    rp1[z] = pairs[...]
+    rp1[q] = pairs[...]
 
     tile_row = lax.broadcasted_iota(jnp.int32, (8, 128), 0)
     rhs[...] = jnp.zeros_like(rhs)
     s4[...] = jnp.zeros_like(s4)
     tail[...] = jnp.zeros_like(tail)
     love_rows[...] = jnp.zeros_like(love_rows)
-    arrive(copies_pz)
+    arrive(copies_pq)
     gathered = rp1[0]
     for i in range(1, 8):
         gathered = jnp.where(tile_row == i, rp1[i], gathered)
-    mine = pl.ds(pl.multiple_of(8 * q, 8), 8)
-    rp2[mine, :] = gathered
-    copies_pq = send(FAR_FIRST, q, 8, q_device, lambda to, d: rp2.at[mine], lambda d: rp2.at[mine], sem_pq)
+    rp2[z] = gathered
+    copies_pz = send(FAR_FIRST, z, 8, z_device, lambda to, d: rp2.at[z], lambda d: rp2.at[z], sem_pz)
 
     pair_lane = pairs[0:1, :]
     love_copy.wait()
@@ -177,8 +181,9 @@
     other = jnp.where(group == 0, 4, 8 - group)
     residue = jnp.where(place % 128 < 64, group, other)
     wanted = (8 * (place % 64) + jnp.where(place < 512, residue, 7 - residue)).astype(F32)
-    arrive(copies_pq)
-    spread = jnp.broadcast_to(rp2[...].reshape(64, 1, 128), (64, 8, 128))
+    arrive(copies_pz)
+    spread = jnp.concatenate([rp2[:, i:i + 1, :] for i in range(8)], axis=0)
+    spread = jnp.broadcast_to(spread, (64, 8, 128))
     diagonal = (tile_row == lane).reshape(1, 8, 128)
     column = jnp.sum(jnp.where(diagonal, spread, 0.0), axis=2, keepdims=True).reshape(512, 1)
     onehot[...] = jnp.where(column == wanted, 1.0, 0.0).astype(BF16)
@@ -243,6 +248,7 @@
         copies2 += send(
             [d for d in part if d], q, 8, q_device, lambda to, d: s2.at[d], lambda d: r2.at[d], sem2
         )
+    settle(7)
     arrive(copies2)
     total = s2[0]
     for d in range(1, 8):
@@ -254,6 +260,7 @@
     quad_copy.wait()
     leg_copy.wait()
     tail[0:8, :] = leg[8192:8200, :].astype(F32)
+    settle(7)
     arrive(copies3)
     for r in range(2):
         for o in range(2):
@@ -278,45 +285,33 @@
             picked = jnp.where(is_low, piece[16 * r:16 * r + 8], piece[16 * r + 8:16 * r + 16])
         return jnp.sum(jnp.where(own_slot, picked, 0.0), axis=0, keepdims=True)
 
-    def chunk_rows(chunk):
-        return pl.ds(pl.multiple_of(2048 * chunk, 2048), 2048)
-
     product = lax.dot_general(fourier, tail_rows, (((1,), (1,)), ((), ())), preferred_element_type=F32)
     for r in range(2):
-        summed = analysed(product, None, r)
-        for d in range(4):
-            s4[d, 32 + r:33 + r, :] = summed
+        s4[0, 32 + r:33 + r, :] = analysed(product, None, r)
     copies4 = []
-    for d in (2, 1, 3, 0):
-        chunk = (x + d) % 4
+    for chunk in range(4):
         product = lax.dot_general(
-            fourier, leg[chunk_rows(chunk), :], (((1,), (1,)), ((), ())), preferred_element_type=F32
+            fourier, leg[2048 * chunk:2048 * chunk + 2048, :], (((1,), (1,)), ((), ())), preferred_element_type=F32
         )
         for row in range(16):
             is_low = jnp.broadcast_to(16 * (16 * chunk + row) < low_limit, (8, 128))
             for r in range(2):
-                s4[d, 16 * r + row:16 * r + row + 1, :] = analysed(product[:, 128 * row:128 * row + 128], is_low, r)
-        if d:
-            copies4 += send((d,), x, 4, x_device, lambda to, d: s4.at[d], lambda d: r4.at[d], sem4)
-
-    arrive(copies4)
-    total = s4[0] + r4[1] + r4[2] + r4[3]
-    own_factor = factor[pl.ds(pl.multiple_of(16 * x, 16), 16), :]
-    scaled = jnp.concatenate([total[0:16] * own_factor, total[16:32] * own_factor], axis=0)
-    r5[0] = scaled.astype(BF16)
-    copies5 = send((2, 1, 3), x, 4, x_device, lambda to, d: r5.at[0], lambda d: r5.at[d], sem5)
-    last_scaled = (total[32:40] * factor[64:65, :]).astype(BF16).astype(F32)
-
-    pieces = []
-    for r in range(2):
-        line = jnp.where(own_slot, jnp.broadcast_to(last_scaled[r:r + 1], (8, 128)), 0.0)
-        pieces += [jnp.zeros((8, 128), F32), line]
-    profile = jnp.dot(jnp.concatenate(pieces, axis=0).astype(BF16), tail_rows, preferred_element_type=F32)
-    for d in (0, 1, 3, 2):
-        if d:
-            arrive([copies5[(2, 1, 3).index(d)]])
-        chunk = (x - d + 4) % 4
-        spectral = r5[d].astype(F32)
+                s4[chunk, 16 * r + row:16 * r + row + 1, :] = analysed(
+                    product[:, 128 * row:128 * row + 128], is_low, r
+                )
+        size = 32 if chunk else 40
+        copies4.append(send(
+            (2, 1, 3), x, 4, x_device,
+            lambda to, d: s4.at[chunk, pl.ds(0, size)], lambda d: r4.at[d, chunk, pl.ds(0, size)], sem4.at[chunk],
+        ))
+
+    settle(12)
+    profile = jnp.zeros((32, 256), F32)
+    for chunk in range(4):
+        arrive(copies4[chunk])
+        total = s4[chunk] + r4[1, chunk] + r4[2, chunk] + r4[3, chunk]
+        scale = factor[16 * chunk:16 * chunk + 16, :]
+        spectral = jnp.concatenate([total[0:16] * scale, total[16:32] * scale], axis=0).astype(BF16).astype(F32)
         for row in range(16):
             is_low = jnp.broadcast_to(16 * (16 * chunk + row) < low_limit, (8, 128))
             pieces = []
@@ -324,8 +319,19 @@
                 line = jnp.broadcast_to(spectral[16 * r + row:16 * r + row + 1], (8, 128))
                 line = jnp.where(own_slot, line, 0.0)
                 pieces += [jnp.where(is_low, line, 0.0), jnp.where(is_low, 0.0, line)]
-            blocks[d, :, 128 * row:128 * row + 128] = jnp.concatenate(pieces, axis=0).astype(BF16)
-        profile = profile + jnp.dot(blocks[d], leg[chunk_rows(chunk), :], preferred_element_type=F32)
+            blocks[chunk, :, 128 * row:128 * row + 128] = jnp.concatenate(pieces, axis=0).astype(BF16)
+        profile = profile + jnp.dot(
+            blocks[chunk], leg[2048 * chunk:2048 * chunk + 2048, :], preferred_element_type=F32
+        )
+        if chunk == 0:
+            last = (total[32:40] * factor[64:65, :]).astype(BF16).astype(F32)
+            pieces = []
+            for r in range(2):
+                line = jnp.where(own_slot, jnp.broadcast_to(last[r:r + 1], (8, 128)), 0.0)
+                pieces += [jnp.zeros((8, 128), F32), line]
+            profile = profile + jnp.dot(
+                jnp.concatenate(pieces, axis=0).astype(BF16), tail_rows, preferred_element_type=F32
+            )
     profile = profile.astype(BF16).astype(F32)
 
     for h in range(2):
@@ -339,10 +345,12 @@
             s6[4 * h + g] = tile
     copies6 = send(FAR_FIRST, z, 8, z_device, lambda to, d: s6.at[to], lambda d: r6.at[z], sem6)
     r6[z] = s6[z]
+    settle(7)
     arrive(copies6)
 
     r7[q] = r6[...].reshape(64, 128).astype(BF16)
     copies7 = send(FAR_FIRST, q, 8, q_device, lambda to, d: r7.at[q], lambda d: r7.at[q], sem7)
+    settle(7)
     arrive(copies7)
     natural = lax.dot_general(
         r7[...].reshape(512, 128), onehot[...], (((0,), (0,)), ((), ())), preferred_element_type=F32
@@ -384,24 +392,23 @@
     for i, value in enumerate((b0 + a0, b1 + a1, b2 + a2, b3 + a3, b0 - a0, b1 - a1, b2 - a2, b3 - a3)):
         s8[i] = (2.0 * value).astype(BF16)
 
-    copies8 = send(FAR_FIRST, z, 8, z_device, lambda to, d: s8.at[to], lambda d: r8.at[z], sem8)
-    r8[z] = s8[z]
+    copies8 = send(FAR_FIRST, z, 8, z_device, lambda to, d: s8.at[to], lambda d: out.at[z], sem8)
+    own_copy = pltpu.make_async_copy(s8.at[z], out.at[z], local_sem.at[6])
+    own_copy.start()
+    settle(7)
     arrive(copies8)
-    grid = r8[...].reshape(256, 256).astype(F32).T
-    out[...] = grid[0:135, :]
-    for copy in started:
-        copy.wait_send()
+    own_copy.wait()
+    settle()
 
 
 def per_device(field, quad_weight, legendre, love_factor, pair_table):
-    vmem = pl.BlockSpec(memory_space=pltpu.VMEM)
     anywhere = pl.BlockSpec(memory_space=pl.ANY)
     pair_sems = pltpu.SemaphoreType.DMA((2, 8))
     grid = pl.pallas_call(
         kernel,
-        out_shape=jax.ShapeDtypeStruct((LON_COLS, 256), F32),
+        out_shape=jax.ShapeDtypeStruct((8, 32, 256), BF16),
         in_specs=[anywhere] * 6,
-        out_specs=vmem,
+        out_specs=anywhere,
         scratch_shapes=[
             pltpu.VMEM((LON_COLS, 256), F32),
             pltpu.VMEM((1, 256), F32),
@@ -415,7 +422,7 @@
             pltpu.VMEM((8, 40, 128), F32),
             pltpu.VMEM((8, 40, 128), F32),
             pltpu.VMEM((8, 8, 128), F32),
-            pltpu.VMEM((64, 128), F32),
+            pltpu.VMEM((8, 8, 128), F32),
             pltpu.VMEM((512, 1024), BF16),
             pltpu.VMEM((4, 256, 128), F32),
             pltpu.VMEM((1024, 128), F32),
@@ -425,8 +432,7 @@
             pltpu.VMEM((8, 8, 128), F32),
             pltpu.VMEM((32, 256), F32),
             pltpu.VMEM((4, 40, 128), F32),
-            pltpu.VMEM((4, 40, 128), F32),
-            pltpu.VMEM((4, 32, 128), BF16),
+            pltpu.VMEM((4, 4, 40, 128), F32),
             pltpu.VMEM((72, 128), F32),
             pltpu.VMEM((16, 128), F32),
             pltpu.VMEM((4, 32, 2048), BF16),
@@ -434,9 +440,8 @@
             pltpu.VMEM((8, 8, 128), F32),
             pltpu.VMEM((8, 64, 128), BF16),
             pltpu.VMEM((8, 32, 256), BF16),
-            pltpu.VMEM((8, 32, 256), BF16),
-            pltpu.SemaphoreType.DMA((6,)),
-        ] + [pair_sems] * 10,
+            pltpu.SemaphoreType.DMA((7,)),
+        ] + [pair_sems] * 8 + [pltpu.SemaphoreType.DMA((4, 2, 4))],
         compiler_params=pltpu.CompilerParams(
             collective_id=0, has_side_effects=True, vmem_limit_bytes=60 * 1024 * 1024
         ),
@@ -448,7 +453,7 @@
         legendre.transpose(1, 0, 2).reshape(8200, 256),
         jnp.asarray(angle_constants()),
     )
-    return grid.T
+    return grid.reshape(256, 256)[:, :LON_COLS].astype(F32)
 
 
 def solution(mesh):

time: 56.2 us -> 51.7 us (0.920)
  Pallas kernels: 54.5 us -> 49.9 us
  other arithmetic: 0 us -> 0.67 us
  local copies, waits for them, and re-layouts: 1.57 us -> 1 us
    pallas_call x1, Pallas kernels: 54.5 us -> 49.9 us  [per_device(): pl.pallas_call(kernel, out_shape=jax.ShapeDtypeStruct((8, 32, 256), BF16)...]
    convert_element_type x0 -> x1, other arithmetic: none -> 0.67 us  [per_device(): return grid.reshape(256, 256)[:, :LON_COLS].astype(F32)]
    unnamed x1, local copies, waits for them, and re-layouts: 1.57 us -> 1 us
where the time goes in v3:
time: 51.7 us; the launch traced here: 51.6 us
  Pallas kernels  49.9 us (97%)
  local copies, waits for them, and re-layouts  1 us (2%)
  other arithmetic  0.67 us (1%)
    pallas_call x1, Pallas kernels, per_device(): pl.pallas_call(kernel, out_shape=jax.ShapeDtypeStruct((8, 32, 256), BF16)...  49.9 us

profile of v3, /device:TPU:1, one launch (start us, length us, event | category | flops | bytes accessed | tf_op | source)
XLA Modules:
  0.0 51.6 jit_solution(8832836837392837479)
XLA Ops:
  0.0 49.9 %shard_map.64 = bf16[8,32,256]{2,1,0:T(8,128)(2,1)} custom-call(f32[135,256]{1,0:T(8,128)} %bitcast.11, f32[1,256]{1,0:T(1,128)} %bitcast.13, f32[8,128]{1,0:T(8,128)} %bitcast.12, s32[1,8]{1,0:T(1,128)} %bitcast.14, bf16[8200,256]{1,0:T(8,128)(2,1)} %bitcast.9, bf16[8,4,2,512,256]{4,3,2,1,0:T(8,128)(2,1)} %constant.2.clone.angles), custom_call_target="tpu_custom_call" | custom-call | tf_op jit(solution)/shard_map/pallas_call | solution.py:407
  49.9 1.0 %copy.8 = bf16[256,135]{0,1:T(8,128)(2,1)S(1)} copy(bf16[256,135]{1,0:T(8,128)(2,1)} %bitcast.10) | data formatting | bytes 138240
  50.9 0.7 %convert_element_type.3 = f32[256,135]{0,1:T(8,128)} convert(bf16[256,135]{0,1:T(8,128)(2,1)S(1)} %copy.8) | non-fusion elementwise | flops 34560 | bytes 207360 | tf_op jit(solution)/shard_map/convert_element_type | solution.py:456

commit v4 on v3

--- a/solution.py
+++ b/solution.py
@@ -107,6 +107,12 @@
         for copy in copies:
             copy.wait_recv()
 
+    def arrived(target, sems, d):
+        pltpu.make_async_remote_copy(
+            src_ref=target, dst_ref=target, send_sem=sems.at[0, d], recv_sem=sems.at[1, d],
+            device_id=z_device((z + d) % 8),
+        ).wait_recv()
+
     lane = lax.broadcasted_iota(jnp.int32, (1, 128), 1)
     quarter = lane // 32
     step_in_tile = lane // 8
@@ -145,7 +151,7 @@
     for i in range(1, 8):
         gathered = jnp.where(tile_row == i, rp1[i], gathered)
     rp2[z] = gathered
-    copies_pz = send(FAR_FIRST, z, 8, z_device, lambda to, d: rp2.at[z], lambda d: rp2.at[z], sem_pz)
+    send(FAR_FIRST, z, 8, z_device, lambda to, d: rp2.at[z], lambda d: rp2.at[z], sem_pz)
 
     pair_lane = pairs[0:1, :]
     love_copy.wait()
@@ -181,12 +187,7 @@
     other = jnp.where(group == 0, 4, 8 - group)
     residue = jnp.where(place % 128 < 64, group, other)
     wanted = (8 * (place % 64) + jnp.where(place < 512, residue, 7 - residue)).astype(F32)
-    arrive(copies_pz)
-    spread = jnp.concatenate([rp2[:, i:i + 1, :] for i in range(8)], axis=0)
-    spread = jnp.broadcast_to(spread, (64, 8, 128))
-    diagonal = (tile_row == lane).reshape(1, 8, 128)
-    column = jnp.sum(jnp.where(diagonal, spread, 0.0), axis=2, keepdims=True).reshape(512, 1)
-    onehot[...] = jnp.where(column == wanted, 1.0, 0.0).astype(BF16)
+    diagonal = lax.broadcasted_iota(jnp.int32, (16, 128), 0) % 8 == lane
 
     table_copy.wait()
     arrive(copies1)
@@ -237,31 +238,61 @@
     value = orders_all[...]
     head = value.astype(BF16)
     rest = (value - head.astype(F32)).astype(BF16)
+
+    odd = z % 2
+    near_other = 2 + 4 * odd
+    far_other = 6 - 4 * odd
+
+    def plane_pair(half, i):
+        return (z // 2 + odd + 3 + 2 * half + i) % 4
+
     copies2 = []
-    for part in ((4, 3, 5, 2), (6, 1, 7, 0)):
-        rows = jnp.concatenate(
-            [onehot[pl.ds(pl.multiple_of((q + d) % 8 * 64, 64), 64), :] for d in part], axis=0
+    for half in range(2):
+        for d in ((1, 7, near_other), (3, 4, 5, far_other))[half]:
+            arrived(rp2.at[z], sem_pz, d)
+        columns = []
+        for i in range(2):
+            first, second = rp2[2 * plane_pair(half, i)], rp2[2 * plane_pair(half, i) + 1]
+            for to in range(8):
+                both = jnp.concatenate([
+                    jnp.broadcast_to(first[to:to + 1], (8, 128)), jnp.broadcast_to(second[to:to + 1], (8, 128))
+                ], axis=0)
+                columns.append(jnp.sum(jnp.where(diagonal, both, 0.0), axis=1, keepdims=True))
+        for i in range(2):
+            for to in range(8):
+                at = pl.multiple_of(64 * to + 16 * plane_pair(half, i), 16)
+                onehot[pl.ds(at, 16), :] = jnp.where(columns[8 * i + to] == wanted, 1.0, 0.0).astype(BF16)
+        rows = jnp.concatenate([
+            onehot[pl.ds(pl.multiple_of((q + d) % 8 * 64 + 16 * plane_pair(half, i), 16), 16), :]
+            for d in range(8) for i in range(2)
+        ], axis=0)
+        in_slots = jnp.dot(rows, head, preferred_element_type=F32) + jnp.dot(rows, rest, preferred_element_type=F32)
+        s2[half] = in_slots.reshape(8, 32, 128)
+        copies2.append(send(
+            FAR_FIRST, q, 8, q_device, lambda to, d: s2.at[half, d], lambda d: r2.at[half, d], sem2.at[half]
+        ))
+    settle(14)
+
+    for half in range(2):
+        arrive(copies2[half])
+        total = s2[half, 0]
+        for d in range(1, 8):
+            total = total + r2[half, d]
+        for i in range(2):
+            for plane in range(2):
+                s3[2 * plane_pair(half, i) + plane] = total[16 * i + 8 * plane:16 * i + 8 * plane + 8]
+        send(
+            ((7, 1, far_other), (4, 3, 5, near_other))[half], z, 8, z_device,
+            lambda to, d: s3.at[to], lambda d: r3.at[z], sem3,
         )
-        in_slots = jnp.dot(rows, head, preferred_element_type=F32) + jnp.dot(rows, rest, preferred_element_type=F32)
-        for i, d in enumerate(part):
-            s2[d] = in_slots[64 * i:64 * i + 64]
-        copies2 += send(
-            [d for d in part if d], q, 8, q_device, lambda to, d: s2.at[d], lambda d: r2.at[d], sem2
-        )
-    settle(7)
-    arrive(copies2)
-    total = s2[0]
-    for d in range(1, 8):
-        total = total + r2[d]
-
-    s3[...] = total.reshape(8, 8, 128)
-    copies3 = send(FAR_FIRST, z, 8, z_device, lambda to, d: s3.at[to], lambda d: r3.at[z], sem3)
     r3[z] = s3[z]
+
     quad_copy.wait()
     leg_copy.wait()
     tail[0:8, :] = leg[8192:8200, :].astype(F32)
     settle(7)
-    arrive(copies3)
+    for d in range(1, 8):
+        arrived(r3.at[z], sem3, d)
     for r in range(2):
         for o in range(2):
             j = 2 * o + r
@@ -426,8 +457,8 @@
             pltpu.VMEM((512, 1024), BF16),
             pltpu.VMEM((4, 256, 128), F32),
             pltpu.VMEM((1024, 128), F32),
-            pltpu.VMEM((8, 64, 128), F32),
-            pltpu.VMEM((8, 64, 128), F32),
+            pltpu.VMEM((2, 8, 32, 128), F32),
+            pltpu.VMEM((2, 8, 32, 128), F32),
             pltpu.VMEM((8, 8, 128), F32),
             pltpu.VMEM((8, 8, 128), F32),
             pltpu.VMEM((32, 256), F32),
@@ -441,7 +472,7 @@
             pltpu.VMEM((8, 64, 128), BF16),
             pltpu.VMEM((8, 32, 256), BF16),
             pltpu.SemaphoreType.DMA((7,)),
-        ] + [pair_sems] * 8 + [pltpu.SemaphoreType.DMA((4, 2, 4))],
+        ] + [pair_sems] * 3 + [pltpu.SemaphoreType.DMA((2, 2, 8))] + [pair_sems] * 4 + [pltpu.SemaphoreType.DMA((4, 2, 4))],
         compiler_params=pltpu.CompilerParams(
             collective_id=0, has_side_effects=True, vmem_limit_bytes=60 * 1024 * 1024
         ),

time: 51.7 us -> 50.2 us (0.971)
  Pallas kernels: 49.9 us -> 48.4 us
    pallas_call x1, Pallas kernels: 49.9 us -> 48.4 us  [per_device(): pl.pallas_call(kernel, out_shape=jax.ShapeDtypeStruct((8, 32, 256), BF16)...]
where the time goes in v4:
time: 50.2 us; the launch traced here: 50.1 us
  Pallas kernels  48.4 us (96%)
  local copies, waits for them, and re-layouts  1 us (2%)
  other arithmetic  0.67 us (1%)
    pallas_call x1, Pallas kernels, per_device(): pl.pallas_call(kernel, out_shape=jax.ShapeDtypeStruct((8, 32, 256), BF16)...  48.4 us

profile of v4, /device:TPU:1, one launch (start us, length us, event | category | flops | bytes accessed | tf_op | source)
XLA Modules:
  0.0 50.1 jit_solution(3759540482731919745)
XLA Ops:
  0.0 48.4 %shard_map.64 = bf16[8,32,256]{2,1,0:T(8,128)(2,1)} custom-call(f32[135,256]{1,0:T(8,128)} %bitcast.11, f32[1,256]{1,0:T(1,128)} %bitcast.13, f32[8,128]{1,0:T(8,128)} %bitcast.12, s32[1,8]{1,0:T(1,128)} %bitcast.14, bf16[8200,256]{1,0:T(8,128)(2,1)} %bitcast.9, bf16[8,4,2,512,256]{4,3,2,1,0:T(8,128)(2,1)} %constant.2.clone.angles), custom_call_target="tpu_custom_call" | custom-call | tf_op jit(solution)/shard_map/pallas_call | solution.py:438
  48.4 1.0 %copy.8 = bf16[256,135]{0,1:T(8,128)(2,1)S(1)} copy(bf16[256,135]{1,0:T(8,128)(2,1)} %bitcast.10) | data formatting | bytes 138240
  49.4 0.7 %convert_element_type.3 = f32[256,135]{0,1:T(8,128)} convert(bf16[256,135]{0,1:T(8,128)(2,1)S(1)} %copy.8) | non-fusion elementwise | flops 34560 | bytes 207360 | tf_op jit(solution)/shard_map/convert_element_type | solution.py:487

commit v5 on v4

--- a/solution.py
+++ b/solution.py
@@ -49,7 +49,7 @@
 def kernel(
     field_in, quad_in, love_in, pair_in, legendre, angles, out,
     field, quad, love, pair_own, pairs, leg, table, tail, last_rows, s1, r1, rp1, rp2, onehot, rhs, orders_all, s2, r2, s3, r3, four, s4, r4,
-    factor, love_rows, blocks, s6, r6, r7, s8,
+    factor, love_rows, spectral, blocks, s6, r6, r7, s8,
     local_sem, sem_pz, sem_pq, sem1, sem2, sem3, sem6, sem7, sem8, sem4,
 ):
     lon = lax.axis_index("lon")
@@ -59,6 +59,14 @@
 
     def z_device(i):
         return {"lon": i * 8 + q}
+
+    y = q // 2
+    core = q % 2
+
+    def zy_device(i, j):
+        return {"lon": i * 8 + 2 * j + core}
+
+    other_core = {"lon": z * 8 + 2 * y + 1 - core}
 
     def q_device(i):
         return {"lon": z * 8 + i}
@@ -84,6 +92,20 @@
         copy.start()
 
     unsettled = []
+
+    def send_one(source, target, send_sem, recv_sem, device):
+        copy = pltpu.make_async_remote_copy(
+            src_ref=source, dst_ref=target, send_sem=send_sem, recv_sem=recv_sem, device_id=device
+        )
+        copy.start()
+        unsettled.append(copy)
+        return copy
+
+    def arrived_zy(target, sems, dz, dy):
+        pltpu.make_async_remote_copy(
+            src_ref=target, dst_ref=target, send_sem=sems.at[0, dz, dy], recv_sem=sems.at[1, dz, dy],
+            device_id=zy_device((z + 1) % 8, y),
+        ).wait_recv()
 
     def send(distances, me, size, device, source, target, sems):
         copies = []
@@ -233,11 +255,10 @@
             rows = (plain[0:64], other[64:128], plain[128:192], other[192:256])
         for half in range(2):
             at = 128 * g + 64 * half
-            orders_all[at:at + 64, :] = jnp.where(lane < 64, rows[half], 0.0)
-            orders_all[512 + at:512 + at + 64, :] = jnp.where(lane < 64, 0.0, turned(rows[2 + half], 64))
-    value = orders_all[...]
-    head = value.astype(BF16)
-    rest = (value - head.astype(F32)).astype(BF16)
+            for o in range(2):
+                value = rows[2 * o + half]
+                head = value.astype(BF16).astype(F32)
+                orders_all[o, at:at + 64, :] = jnp.where(lane < 64, head, turned(value - head, 64)).astype(BF16)
 
     odd = z % 2
     near_other = 2 + 4 * odd
@@ -263,44 +284,55 @@
                 at = pl.multiple_of(64 * to + 16 * plane_pair(half, i), 16)
                 onehot[pl.ds(at, 16), :] = jnp.where(columns[8 * i + to] == wanted, 1.0, 0.0).astype(BF16)
         rows = jnp.concatenate([
-            onehot[pl.ds(pl.multiple_of((q + d) % 8 * 64 + 16 * plane_pair(half, i), 16), 16), :]
-            for d in range(8) for i in range(2)
+            onehot[pl.ds(pl.multiple_of(
+                64 * (2 * ((y + dy) % 4) + (core + e) % 2) + 16 * plane_pair(half, i), 16
+            ), 16), :]
+            for e in range(2) for dy in range(4) for i in range(2)
         ], axis=0)
-        in_slots = jnp.dot(rows, head, preferred_element_type=F32) + jnp.dot(rows, rest, preferred_element_type=F32)
-        s2[half] = in_slots.reshape(8, 32, 128)
-        copies2.append(send(
-            FAR_FIRST, q, 8, q_device, lambda to, d: s2.at[half, d], lambda d: r2.at[half, d], sem2.at[half]
+        low_part = jnp.dot(rows[:, 0:512], orders_all[0], preferred_element_type=F32)
+        high_part = jnp.dot(rows[:, 512:1024], orders_all[1], preferred_element_type=F32)
+        in_slots = jnp.where(lane < 64, low_part + turned(low_part, 64), high_part + turned(high_part, 64))
+        s2[half] = in_slots.reshape(2, 128, 128)
+        copies2.append(send_one(
+            s2.at[half, 1], r2.at[half], sem2.at[0, half], sem2.at[1, half], other_core
         ))
-    settle(14)
+    settle(2)
 
     for half in range(2):
-        arrive(copies2[half])
-        total = s2[half, 0]
-        for d in range(1, 8):
-            total = total + r2[half, d]
-        for i in range(2):
-            for plane in range(2):
-                s3[2 * plane_pair(half, i) + plane] = total[16 * i + 8 * plane:16 * i + 8 * plane + 8]
-        send(
-            ((7, 1, far_other), (4, 3, 5, near_other))[half], z, 8, z_device,
-            lambda to, d: s3.at[to], lambda d: r3.at[z], sem3,
-        )
-    r3[z] = s3[z]
+        copies2[half].wait_recv()
+        total = s2[half, 0] + r2[half]
+        for dy in range(4):
+            for i in range(2):
+                for plane in range(2):
+                    at = 32 * dy + 16 * i + 8 * plane
+                    s3[dy, 2 * plane_pair(half, i) + plane] = total[at:at + 8]
+        for dz in ((far_other, 1, 7, 0), (4, 3, 5, near_other))[half]:
+            for dy in (2, 1, 3, 0):
+                if isinstance(dz, int) and dz == 0 and dy == 0:
+                    continue
+                send_one(
+                    s3.at[dy, (z + dz) % 8], r3.at[y, z], sem3.at[0, dz, dy], sem3.at[1, dz, dy],
+                    zy_device((z + dz) % 8, (y + dy) % 4),
+                )
+    r3[y, z] = s3[0, z]
 
     quad_copy.wait()
     leg_copy.wait()
     tail[0:8, :] = leg[8192:8200, :].astype(F32)
-    settle(7)
-    for d in range(1, 8):
-        arrived(r3.at[z], sem3, d)
+    settle(31)
+    for dz in range(8):
+        for dy in range(4):
+            if dz or dy:
+                arrived_zy(r3.at[y, z], sem3, dz, dy)
+    own_sums = [r3[0, i] + r3[1, i] + r3[2, i] + r3[3, i] for i in range(8)]
     for r in range(2):
         for o in range(2):
             j = 2 * o + r
             for h in range(2):
                 cols = slice(128 * h, 128 * h + 128)
-                tile = turned(r3[4 * h], -32 * j)
+                tile = turned(own_sums[4 * h], -32 * j)
                 for g in range(1, 4):
-                    tile = jnp.where(quarter == g, turned(r3[4 * h + g], 32 * (g - j)), tile)
+                    tile = jnp.where(quarter == g, turned(own_sums[4 * h + g], 32 * (g - j)), tile)
                 at = 16 * r + 8 * o
                 four[at:at + 8, cols] = tile / float(TOTAL_LON) * quad[0:1, cols]
     fourier = four[...].astype(BF16)
@@ -342,12 +374,12 @@
         arrive(copies4[chunk])
         total = s4[chunk] + r4[1, chunk] + r4[2, chunk] + r4[3, chunk]
         scale = factor[16 * chunk:16 * chunk + 16, :]
-        spectral = jnp.concatenate([total[0:16] * scale, total[16:32] * scale], axis=0).astype(BF16).astype(F32)
+        spectral[chunk] = jnp.concatenate([total[0:16] * scale, total[16:32] * scale], axis=0).astype(BF16).astype(F32)
         for row in range(16):
             is_low = jnp.broadcast_to(16 * (16 * chunk + row) < low_limit, (8, 128))
             pieces = []
             for r in range(2):
-                line = jnp.broadcast_to(spectral[16 * r + row:16 * r + row + 1], (8, 128))
+                line = jnp.broadcast_to(spectral[chunk, 16 * r + row:16 * r + row + 1, :], (8, 128))
                 line = jnp.where(own_slot, line, 0.0)
                 pieces += [jnp.where(is_low, line, 0.0), jnp.where(is_low, 0.0, line)]
             blocks[chunk, :, 128 * row:128 * row + 128] = jnp.concatenate(pieces, axis=0).astype(BF16)
@@ -374,14 +406,27 @@
                     quarter == j, turned(profile[at:at + 8, 128 * h:128 * h + 128], 32 * (j - g)), tile
                 )
             s6[4 * h + g] = tile
-    copies6 = send(FAR_FIRST, z, 8, z_device, lambda to, d: s6.at[to], lambda d: r6.at[z], sem6)
-    r6[z] = s6[z]
-    settle(7)
-    arrive(copies6)
-
-    r7[q] = r6[...].reshape(64, 128).astype(BF16)
-    copies7 = send(FAR_FIRST, q, 8, q_device, lambda to, d: r7.at[q], lambda d: r7.at[q], sem7)
-    settle(7)
+    for dz in FAR_FIRST + (0,):
+        for dy in (2, 1, 3, 0):
+            if dz or dy:
+                send_one(
+                    s6.at[(z + dz) % 8], r6.at[y, z], sem6.at[0, dz, dy], sem6.at[1, dz, dy],
+                    zy_device((z + dz) % 8, (y + dy) % 4),
+                )
+    r6[y, z] = s6[z]
+    settle(31)
+
+    copies7 = []
+    for dy in (0, 1, 3, 2):
+        for dz in range(8):
+            if dz or dy:
+                arrived_zy(r6.at[y, z], sem6, dz, dy)
+        row = (y - dy + 4) % 4
+        r7[row, core] = r6[row].reshape(64, 128).astype(BF16)
+        copies7.append(send_one(
+            r7.at[row, core], r7.at[row, core], sem7.at[0, dy], sem7.at[1, dy], other_core
+        ))
+    settle(4)
     arrive(copies7)
     natural = lax.dot_general(
         r7[...].reshape(512, 128), onehot[...], (((0,), (0,)), ((), ())), preferred_element_type=F32
@@ -435,6 +480,8 @@
 def per_device(field, quad_weight, legendre, love_factor, pair_table):
     anywhere = pl.BlockSpec(memory_space=pl.ANY)
     pair_sems = pltpu.SemaphoreType.DMA((2, 8))
+    plane_sems = pltpu.SemaphoreType.DMA((2, 8, 4))
+    core_sems = pltpu.SemaphoreType.DMA((2, 4))
     grid = pl.pallas_call(
         kernel,
         out_shape=jax.ShapeDtypeStruct((8, 32, 256), BF16),
@@ -456,23 +503,24 @@
             pltpu.VMEM((8, 8, 128), F32),
             pltpu.VMEM((512, 1024), BF16),
             pltpu.VMEM((4, 256, 128), F32),
-            pltpu.VMEM((1024, 128), F32),
-            pltpu.VMEM((2, 8, 32, 128), F32),
-            pltpu.VMEM((2, 8, 32, 128), F32),
-            pltpu.VMEM((8, 8, 128), F32),
-            pltpu.VMEM((8, 8, 128), F32),
+            pltpu.VMEM((2, 512, 128), BF16),
+            pltpu.VMEM((2, 2, 128, 128), F32),
+            pltpu.VMEM((2, 128, 128), F32),
+            pltpu.VMEM((4, 8, 8, 128), F32),
+            pltpu.VMEM((4, 8, 8, 128), F32),
             pltpu.VMEM((32, 256), F32),
             pltpu.VMEM((4, 40, 128), F32),
             pltpu.VMEM((4, 4, 40, 128), F32),
             pltpu.VMEM((72, 128), F32),
             pltpu.VMEM((16, 128), F32),
+            pltpu.VMEM((4, 32, 128), F32),
             pltpu.VMEM((4, 32, 2048), BF16),
             pltpu.VMEM((8, 8, 128), F32),
-            pltpu.VMEM((8, 8, 128), F32),
-            pltpu.VMEM((8, 64, 128), BF16),
+            pltpu.VMEM((4, 8, 8, 128), F32),
+            pltpu.VMEM((4, 2, 64, 128), BF16),
             pltpu.VMEM((8, 32, 256), BF16),
             pltpu.SemaphoreType.DMA((7,)),
-        ] + [pair_sems] * 3 + [pltpu.SemaphoreType.DMA((2, 2, 8))] + [pair_sems] * 4 + [pltpu.SemaphoreType.DMA((4, 2, 4))],
+        ] + [pair_sems] * 3 + [core_sems, plane_sems, plane_sems, core_sems, pair_sems] + [pltpu.SemaphoreType.DMA((4, 2, 4))],
         compiler_params=pltpu.CompilerParams(
             collective_id=0, has_side_effects=True, vmem_limit_bytes=60 * 1024 * 1024
         ),

time: 50.2 us -> 49.9 us (level)
  no operation moved by 1% of the time
where the time goes in v5:
time: 49.9 us; the launch traced here: 49.8 us
  Pallas kernels  48.1 us (96%)
  local copies, waits for them, and re-layouts  1 us (2%)
  other arithmetic  0.67 us (1%)
    pallas_call x1, Pallas kernels, per_device(): pl.pallas_call(kernel, out_shape=jax.ShapeDtypeStruct((8, 32, 256), BF16)...  48.1 us
    unnamed x1, local copies, waits for them, and re-layouts  1 us

profile of v5, /device:TPU:1, one launch (start us, length us, event | category | flops | bytes accessed | tf_op | source)
XLA Modules:
  0.0 49.8 jit_solution(16035381245451293834)
XLA Ops:
  0.0 48.1 %shard_map.64 = bf16[8,32,256]{2,1,0:T(8,128)(2,1)} custom-call(f32[135,256]{1,0:T(8,128)} %bitcast.11, f32[1,256]{1,0:T(1,128)} %bitcast.13, f32[8,128]{1,0:T(8,128)} %bitcast.12, s32[1,8]{1,0:T(1,128)} %bitcast.14, bf16[8200,256]{1,0:T(8,128)(2,1)} %bitcast.9, bf16[8,4,2,512,256]{4,3,2,1,0:T(8,128)(2,1)} %constant.2.clone.angles), custom_call_target="tpu_custom_call" | custom-call | tf_op jit(solution)/shard_map/pallas_call | solution.py:485
  48.1 1.0 %copy.8 = bf16[256,135]{0,1:T(8,128)(2,1)S(1)} copy(bf16[256,135]{1,0:T(8,128)(2,1)} %bitcast.10) | data formatting | bytes 138240
  49.1 0.7 %convert_element_type.3 = f32[256,135]{0,1:T(8,128)} convert(bf16[256,135]{0,1:T(8,128)(2,1)S(1)} %copy.8) | non-fusion elementwise | flops 34560 | bytes 207360 | tf_op jit(solution)/shard_map/convert_element_type | solution.py:535

commit v6 on v5

--- a/solution.py
+++ b/solution.py
@@ -427,10 +427,16 @@
             r7.at[row, core], r7.at[row, core], sem7.at[0, dy], sem7.at[1, dy], other_core
         ))
     settle(4)
-    arrive(copies7)
-    natural = lax.dot_general(
-        r7[...].reshape(512, 128), onehot[...], (((0,), (0,)), ((), ())), preferred_element_type=F32
-    )
+    natural = jnp.zeros((128, 1024), F32)
+    for e in range(2):
+        if e:
+            arrive(copies7)
+        part = (core + e) % 2
+        left = jnp.concatenate([r7[row, part] for row in range(4)], axis=0)
+        right = jnp.concatenate(
+            [onehot[pl.ds(pl.multiple_of(128 * row + 64 * part, 64), 64), :] for row in range(4)], axis=0
+        )
+        natural = natural + lax.dot_general(left, right, (((0,), (0,)), ((), ())), preferred_element_type=F32)
     wide_lane = lax.broadcasted_iota(jnp.int32, (1, 256), 1)
     second_half = wide_lane % 128 >= 64
     waves = []

time: 49.9 us -> 50 us (level)
  no operation moved by 1% of the time
where the time goes in v6:
time: 50 us; the launch traced here: 49.9 us
  Pallas kernels  48.2 us (96%)
  local copies, waits for them, and re-layouts  1 us (2%)
  other arithmetic  0.67 us (1%)
    pallas_call x1, Pallas kernels, per_device(): pl.pallas_call(kernel, out_shape=jax.ShapeDtypeStruct((8, 32, 256), BF16)...  48.2 us
    unnamed x1, local copies, waits for them, and re-layouts  1 us

profile of v6, /device:TPU:1, one launch (start us, length us, event | category | flops | bytes accessed | tf_op | source)
XLA Modules:
  0.0 49.9 jit_solution(11376718420614565124)
XLA Ops:
  0.0 48.2 %shard_map.64 = bf16[8,32,256]{2,1,0:T(8,128)(2,1)} custom-call(f32[135,256]{1,0:T(8,128)} %bitcast.11, f32[1,256]{1,0:T(1,128)} %bitcast.13, f32[8,128]{1,0:T(8,128)} %bitcast.12, s32[1,8]{1,0:T(1,128)} %bitcast.14, bf16[8200,256]{1,0:T(8,128)(2,1)} %bitcast.9, bf16[8,4,2,512,256]{4,3,2,1,0:T(8,128)(2,1)} %constant.2.clone.angles), custom_call_target="tpu_custom_call" | custom-call | tf_op jit(solution)/shard_map/pallas_call | solution.py:491
  48.2 1.0 %copy.8 = bf16[256,135]{0,1:T(8,128)(2,1)S(1)} copy(bf16[256,135]{1,0:T(8,128)(2,1)} %bitcast.10) | data formatting | bytes 138240
  49.2 0.7 %convert_element_type.3 = f32[256,135]{0,1:T(8,128)} convert(bf16[256,135]{0,1:T(8,128)(2,1)S(1)} %copy.8) | non-fusion elementwise | flops 34560 | bytes 207360 | tf_op jit(solution)/shard_map/convert_element_type | solution.py:541
